TPU v7x, 256 devices: a whole 4x4x8 slice. The times are simulated.
256 devices in a mesh: seq: 32 (over z, y), pb: 8 (over x, core).
Axes of the slice: x: 4, y: 4, z: 8, core: 2. Of those that a mesh axis runs over, the one named last changes fastest.
Arguments:
- queries: bfloat16 [8, 4096, 4096], P('pb', 'seq'), may hold values from -6 to 6
- keys: bfloat16 [8, 4096, 1024], P('pb', 'seq'), may hold values from -6 to 6
- values: bfloat16 [8, 4096, 1024], P('pb', 'seq'), may hold values from -18 to 18
- query_gain: float32 [128], replicated, may hold values from 0.1 to 1.9
- key_gain: float32 [128], replicated, may hold values from 0.1 to 1.9
- doc_lengths: int32 [8, 16], P('pb'), may hold values from 1 to 512, 4096 in all within a row
- span_lengths: int32 [8, 128], P('pb'), may hold values from 1 to 64, 4096 in all within a row
- query_emb: bfloat16 [512, 4096], P('pb', 'seq'), may hold values from -0.09375 to 0.09375
- answer_options: int32 [512, 8], replicated, may hold values from 0 to 1023, all different within a row
Outputs:
- query_loss: float32 [512], P('pb')
- query_grad: bfloat16 [8, 4096, 4096], P('pb', 'seq')
- key_grad: bfloat16 [8, 4096, 1024], P('pb', 'seq')
- value_grad: bfloat16 [8, 4096, 1024], P('pb', 'seq')
Inputs may be any that keep to these rules, and one draw needn't show every extreme that they name: `doc_lengths`: row p is the documents of sequence p in order; they sum to 4096, and the longest has exactly 512 tokens. `span_lengths`: row p is the spans of sequence p in order; they sum to 4096, and the longest has exactly 64 tokens. `answer_options`: span p * 128 + c is span c of sequence p. The 8 entries of a row differ; column 0 is the positive. Every span is named by some row.
All inputs are finite; a program needn't handle non-finite values.
Results may differ from a plain program's by a relative error of at most 0.02.
Values may be sent and summed in bfloat16 or wider, within the bound.
A program may use at most 64 MiB of HBM per device.

v0:
```python
import jax
import jax.numpy as jnp
from jax import lax
from jax.sharding import PartitionSpec as P

QUERY_HEADS = 32
KEY_VALUE_HEADS = 8
HEAD_SIZE = 128
DOC_MAX = 512


norm_epsilon = 1e-06
softmax_divisor = 0.05
backprop_factor = 256.0


def segment_index(lengths_row, length):
    first_rows = jnp.cumsum(lengths_row) - lengths_row
    positions = jnp.arange(length, dtype=jnp.int32)
    found = jnp.sum((positions[:, None] >= first_rows[None, :]).astype(jnp.int32), axis=1)
    return (found - 1, first_rows)


def block_window(row_first, first_rows, length, window):
    doc_first = jnp.max(jnp.where(first_rows <= row_first, first_rows, 0))
    return jnp.minimum(doc_first, length - window)


def normalize_rows(entries, gain):
    as_float = entries.astype(jnp.float32)
    recip = lax.rsqrt(jnp.mean(as_float * as_float, axis=-1, keepdims=True) + norm_epsilon)
    return (as_float * recip * gain).astype(jnp.bfloat16)


def normalize_grad(entries, gain, upstream):
    as_float = entries.astype(jnp.float32)
    recip = lax.rsqrt(jnp.mean(as_float * as_float, axis=-1, keepdims=True) + norm_epsilon)
    gained = gain * upstream
    return recip * gained - as_float * recip**3 * jnp.mean(
        as_float * gained, axis=-1, keepdims=True
    )


def attend_forward(normalized_query, normalized_key, single_value_head, doc_ids, first_rows):
    length, heads, width = normalized_query.shape
    rows = min(512, length)
    window = min(rows + 2 * DOC_MAX, length)
    score_scale = width ** (-0.5)

    def one_block(block_index):
        row_first = block_index * rows
        window_first = block_window(row_first, first_rows, length, window)
        query_block = lax.dynamic_slice_in_dim(normalized_query, row_first, rows, 0)
        key_block = lax.dynamic_slice_in_dim(normalized_key, window_first, window, 0)
        value_block = lax.dynamic_slice_in_dim(single_value_head, window_first, window, 0)
        same_doc = (
            lax.dynamic_slice_in_dim(doc_ids, row_first, rows, 0)[:, None]
            == lax.dynamic_slice_in_dim(doc_ids, window_first, window, 0)[None, :]
        )
        scores = (
            jnp.einsum("qhd,kd->hqk", query_block, key_block, preferred_element_type=jnp.float32)
            * score_scale
        )
        weights = jnp.where(same_doc[None], jnp.exp(scores), 0.0)
        totals = jnp.sum(weights, axis=-1)
        probs = (weights / totals[:, :, None]).astype(jnp.bfloat16)
        attended_output = jnp.einsum(
            "hqk,kd->qhd", probs, value_block, preferred_element_type=jnp.float32
        ).astype(jnp.bfloat16)
        return (attended_output, jnp.log(totals).T)

    attended_output, logarithm_totals = lax.map(
        one_block, jnp.arange(length // rows, dtype=jnp.int32)
    )
    return (attended_output.reshape(length, heads, width), logarithm_totals.reshape(length, heads))


def attend_backward(
    normalized_query,
    normalized_key,
    single_value_head,
    attended_output,
    logarithm_totals,
    attn_grad,
    doc_ids,
    first_rows,
):
    length, heads, width = normalized_query.shape
    rows = min(512, length)
    window = min(rows + 2 * DOC_MAX, length)
    score_scale = width ** (-0.5)
    delta = jnp.sum(attn_grad.astype(jnp.float32) * attended_output.astype(jnp.float32), axis=-1)

    def one_block(carry, block_index):
        key_total, value_total = carry
        row_first = block_index * rows
        window_first = block_window(row_first, first_rows, length, window)
        query_block = lax.dynamic_slice_in_dim(normalized_query, row_first, rows, 0)
        key_block = lax.dynamic_slice_in_dim(normalized_key, window_first, window, 0)
        value_block = lax.dynamic_slice_in_dim(single_value_head, window_first, window, 0)
        grad_block = lax.dynamic_slice_in_dim(attn_grad, row_first, rows, 0)
        lse_block = lax.dynamic_slice_in_dim(logarithm_totals, row_first, rows, 0)
        delta_block = lax.dynamic_slice_in_dim(delta, row_first, rows, 0)
        same_doc = (
            lax.dynamic_slice_in_dim(doc_ids, row_first, rows, 0)[:, None]
            == lax.dynamic_slice_in_dim(doc_ids, window_first, window, 0)[None, :]
        )
        scores = (
            jnp.einsum("qhd,kd->hqk", query_block, key_block, preferred_element_type=jnp.float32)
            * score_scale
        )
        recomputed = jnp.where(same_doc[None], jnp.exp(scores - lse_block.T[:, :, None]), 0.0)
        value_part = jnp.einsum(
            "hqk,qhd->kd",
            recomputed.astype(jnp.bfloat16),
            grad_block,
            preferred_element_type=jnp.float32,
        )
        prob_grad = jnp.einsum(
            "qhd,kd->hqk", grad_block, value_block, preferred_element_type=jnp.float32
        )
        score_grad = (recomputed * (prob_grad - delta_block.T[:, :, None]) * score_scale).astype(
            jnp.bfloat16
        )
        query_part = jnp.einsum(
            "hqk,kd->qhd", score_grad, key_block, preferred_element_type=jnp.float32
        )
        key_part = jnp.einsum(
            "hqk,qhd->kd", score_grad, query_block, preferred_element_type=jnp.float32
        )
        key_total = lax.dynamic_update_slice_in_dim(
            key_total,
            lax.dynamic_slice_in_dim(key_total, window_first, window, 0) + key_part,
            window_first,
            0,
        )
        value_total = lax.dynamic_update_slice_in_dim(
            value_total,
            lax.dynamic_slice_in_dim(value_total, window_first, window, 0) + value_part,
            window_first,
            0,
        )
        return ((key_total, value_total), query_part)

    empty = jnp.zeros((length, width), jnp.float32)
    (key_total, value_total), query_parts = lax.scan(
        one_block, (empty, empty), jnp.arange(length // rows, dtype=jnp.int32)
    )
    return (query_parts.reshape(length, heads, width), key_total, value_total)


def on_device(
    queries,
    keys,
    values,
    query_gain,
    key_gain,
    doc_lengths,
    span_lengths,
    query_emb,
    answer_options,
):
    seq_devices = lax.axis_size("seq")
    bank_devices = lax.axis_size("pb")
    tok_rows = queries.shape[1]
    width = HEAD_SIZE
    key_value_heads = KEY_VALUE_HEADS
    group = seq_devices // key_value_heads
    local_heads = QUERY_HEADS // seq_devices
    length = tok_rows * seq_devices
    repeated_keys = jnp.broadcast_to(
        keys[0].reshape(tok_rows, key_value_heads, 1, width),
        (tok_rows, key_value_heads, group, width),
    ).reshape(tok_rows, seq_devices * width)
    repeated_values = jnp.broadcast_to(
        values[0].reshape(tok_rows, key_value_heads, 1, width),
        (tok_rows, key_value_heads, group, width),
    ).reshape(tok_rows, seq_devices * width)
    single_query_head, single_key_head, single_value_head = (
        lax.all_to_all(queries[0], "seq", split_axis=1, concat_axis=0, tiled=True),
        lax.all_to_all(repeated_keys, "seq", split_axis=1, concat_axis=0, tiled=True),
        lax.all_to_all(repeated_values, "seq", split_axis=1, concat_axis=0, tiled=True),
    )
    single_query_head = single_query_head.reshape(length, local_heads, width)
    doc_ids, first_rows = segment_index(doc_lengths[0], length)
    span_ids, span_firsts = segment_index(span_lengths[0], length)
    normalized_query = normalize_rows(single_query_head, query_gain)
    normalized_key = normalize_rows(single_key_head, key_gain)
    attended_output, logarithm_totals = attend_forward(
        normalized_query, normalized_key, single_value_head, doc_ids, first_rows
    )
    span_count = span_lengths.shape[1]
    span_table = (span_ids[None, :] == jnp.arange(span_count, dtype=jnp.int32)[:, None]).astype(
        jnp.bfloat16
    )
    span_sums = jnp.dot(
        span_table,
        attended_output.reshape(length, local_heads * width),
        preferred_element_type=jnp.float32,
    )
    span_sizes = span_lengths[0].astype(jnp.float32)
    span_emb = (span_sums / span_sizes[:, None]).astype(jnp.bfloat16)
    query_count = query_emb.shape[0]
    memory_bank_index = lax.axis_index("pb")
    own_lists = lax.dynamic_slice_in_dim(
        answer_options, memory_bank_index * query_count, query_count, 0
    )
    bank = lax.all_gather(span_emb, "pb", axis=0, tiled=True)
    whole_similarity_matrix = lax.dot_general(
        query_emb, bank, (((1,), (1,)), ((), ())), preferred_element_type=jnp.float32
    )
    running_mixture_vector = jnp.take_along_axis(whole_similarity_matrix, own_lists, axis=1)
    similarity_pool = lax.psum(running_mixture_vector, "seq") / softmax_divisor
    exponentiated_similarities = jnp.exp(similarity_pool)
    similarity_line_sums_per_query = jnp.sum(exponentiated_similarities, axis=1)
    query_loss = jnp.log(similarity_line_sums_per_query) - similarity_pool[:, 0]
    correct_answer_ids = (jnp.arange(answer_options.shape[1], dtype=jnp.int32) == 0).astype(
        jnp.float32
    )
    ranking_objective_factor = (
        backprop_factor
        * (
            exponentiated_similarities / similarity_line_sums_per_query[:, None]
            - correct_answer_ids[None, :]
        )
        / softmax_divisor
    )
    bank_ids = jnp.arange(span_count * bank_devices, dtype=jnp.int32)
    dense = jnp.sum(
        ranking_objective_factor[:, :, None]
        * (own_lists[:, :, None] == bank_ids[None, None, :]).astype(jnp.float32),
        axis=1,
    )
    query_float = query_emb.astype(jnp.float32)
    span_grad = lax.psum_scatter(
        lax.dot_general(
            dense, query_float, (((0,), (0,)), ((), ())), precision=lax.Precision.HIGHEST
        ).astype(jnp.bfloat16),
        "pb",
        scatter_dimension=0,
        tiled=True,
    ).astype(jnp.float32)
    attn_grad = (
        jnp.take(span_grad / span_sizes[:, None], span_ids, axis=0)
        .astype(jnp.bfloat16)
        .reshape(length, local_heads, width)
    )
    normed_qgrad, normed_kgrad, value_total = attend_backward(
        normalized_query,
        normalized_key,
        single_value_head,
        attended_output,
        logarithm_totals,
        attn_grad,
        doc_ids,
        first_rows,
    )
    query_local = (
        normalize_grad(single_query_head, query_gain, normed_qgrad)
        .reshape(length, local_heads * width)
        .astype(jnp.bfloat16)
    )
    key_local = normalize_grad(single_key_head, key_gain, normed_kgrad)
    query_back = lax.all_to_all(query_local, "seq", split_axis=0, concat_axis=1, tiled=True)
    key_back, value_back = (
        lax.all_to_all(
            key_local.astype(jnp.bfloat16), "seq", split_axis=0, concat_axis=1, tiled=True
        ).astype(key_local.dtype),
        lax.all_to_all(
            value_total.astype(jnp.bfloat16), "seq", split_axis=0, concat_axis=1, tiled=True
        ).astype(value_total.dtype),
    )
    key_back = jnp.sum(key_back.reshape(tok_rows, key_value_heads, group, width), axis=2).reshape(
        tok_rows, key_value_heads * width
    )
    value_back = jnp.sum(
        value_back.reshape(tok_rows, key_value_heads, group, width), axis=2
    ).reshape(tok_rows, key_value_heads * width)
    return (
        query_loss,
        query_back[None],
        key_back.astype(jnp.bfloat16)[None],
        value_back.astype(jnp.bfloat16)[None],
    )


def solution(mesh):
    in_specs = (
        P("pb", "seq", None),
        P("pb", "seq", None),
        P("pb", "seq", None),
        P(),
        P(),
        P("pb", None),
        P("pb", None),
        P("pb", "seq"),
        P(),
    )
    out_specs = (P("pb"), P("pb", "seq", None), P("pb", "seq", None), P("pb", "seq", None))
    return jax.shard_map(
        on_device, mesh=mesh, in_specs=in_specs, out_specs=out_specs, check_vma=False
    )
```

profile of v0, /device:TPU:2, one launch (start us, length us, event | category | flops | bytes accessed | tf_op | source)
XLA Modules:
  0.0 650.0 jit_solution(6013083491653238860)
XLA Ops:
  9.5 11.6 %all-to-all-start.2 = ((bf16[128,32,128]{0,2,1:T(8,128)(2,1)}), bf16[128,32,128]{0,2,1:T(8,128)(2,1)S(1)}, u32[]{:S(2)}, u32[]{:S(2)}) async-start(bf16[128,32,128]{0,2,1:T(8,128)(2,1)} %bitcast.35), calls=%async_computation.2 | async-start | bytes 2097152 | tf_op jit(solution)/shard_map/all_to_all | solution.py:180
  22.9 26.3 %all-to-all-done.2 = bf16[128,32,128]{0,2,1:T(8,128)(2,1)S(1)} async-done(((bf16[128,32,128]{0,2,1:T(8,128)(2,1)}), bf16[128,32,128]{0,2,1:T(8,128)(2,1)S(1)}, u32[]{:S(2)}, u32[]{:S(2)}) %all-to-all-start.2) | async-done | bytes 1048608 | tf_op jit(solution)/shard_map/all_to_all | solution.py:180
  50.5 5.5 all-to-all-start.1
  59.3 23.7 %all-to-all-done.1 = bf16[128,32,128]{2,0,1:T(8,128)(2,1)S(1)} async-done(((bf16[128,32,128]{2,0,1:T(8,128)(2,1)}), bf16[128,32,128]{2,0,1:T(8,128)(2,1)S(1)}, u32[]{:S(2)}, u32[]{:S(2)}) %all-to-all-start.1) | async-done | bytes 1048608 | tf_op jit(solution)/shard_map/all_to_all | solution.py:181
  84.3 5.7 all-to-all-start
  97.2 19.3 %all-to-all-done = bf16[128,32,128]{2,0,1:T(8,128)(2,1)} async-done(((bf16[128,32,128]{2,0,1:T(8,128)(2,1)}), bf16[128,32,128]{2,0,1:T(8,128)(2,1)}, u32[]{:S(2)}, u32[]{:S(2)}) %all-to-all-start) | async-done | bytes 1048608 | tf_op jit(solution)/shard_map/all_to_all | solution.py:182
  116.5 54.5 %while.26 = (s32[]{:T(128)}, bf16[8,512,1,128]{1,3,2,0:T(8,128)(2,1)S(1)}, f32[8,512,1]{1,2,0:T(1,128)}, s32[8]{0:T(128)S(1)}, s32[16]{0:T(128)S(1)}, /*index=5*...) while((s32[]{:T(128)}, ...), condition=%wide.region_9.10_spmd, body=%wide.region_6.9_spmd.sunk | while | flops 407436864 | bytes 7377241 | solution.py:72
  172.2 12.9 %all_gather.3 = bf16[1024,128]{1,0:T(8,128)(2,1)S(1)} all-gather(bf16[128,128]{1,0:T(8,128)(2,1)S(1)} %fusion.63), channel_id=1, replica_groups=mesh['seq'=32,'pb'=8] {'pb'}, dimensions={0}, use_global_device_ids=true | all-gather | bytes 294912 | tf_op jit(solution)/shard_map/all_gather | solution.py:208
  185.4 4.5 gather_fusion.1
  190.0 139.6 %psum.7 = f32[64,8]{1,0:T(8,128)S(1)} all-reduce(f32[64,8]{1,0:T(8,128)S(1)} %and_select_fusion), channel_id=1, replica_groups=mesh['seq'=32,'pb'=8] {'seq'}, use_global_device_ids=true, to_apply=%region_10.11 | all-reduce | flops 512 | bytes 4096 | tf_op jit(solution)/shard_map/psum | solution.py:213
  333.5 25.4 %reduce-scatter.2.cloned.1.call-done = bf16[128,128]{1,0:T(8,128)(2,1)} async-done(((bf16[1024,128]{1,0:T(8,128)(2,1)}), bf16[128,128]{1,0:T(8,128)(2,1)}) %reduce-scatter.2.cloned.1.call-update) | async-done | bytes 32784 | tf_op jit(solution)/shard_map/reduce_scatter | solution.py:235
  359.8 15.0 %gather_fusion = bf16[4096,128]{1,0:T(8,128)(2,1)} fusion(bf16[128,128]{1,0:T(8,128)(2,1)S(1)} %convert_divide_fusion, s32[4096]{0:T(1024)S(1)} %broadcast_clamp_fusion), kind=kCustom, calls=%fused_computation | custom fusion | bytes 2113536 | tf_op jit(solution)/shard_map/jit(_take)/gather | solution.py:244
  374.8 3.1 fusion.57
  380.8 157.1 %while.27 = (s32[]{:T(128)}, f32[4096,128]{1,0:T(8,128)}, f32[4096,128]{1,0:T(8,128)}, f32[8,512,1,128]{3,1,0,2:T(8,128)}, s32[8]{0:T(128)S(1)}, /*index=5*/s32[...) while((s32[]{:T(128)}, f32[4096,128]{1,0:T(8,128)}, ...), condition=%wide.region_17.18_spmd, body=%wide.region_15.17_spmd.sunk | while | flops 1014104128 | bytes 23499160 | solution.py:146
  393.0 3.5 dynamic_update_slice.29
  396.5 3.5 dynamic_update_slice.30
  412.9 3.5 dynamic_update_slice.29
  416.4 3.5 dynamic_update_slice.30
  432.8 3.5 dynamic_update_slice.29
  436.3 3.5 dynamic_update_slice.30
  452.8 3.5 dynamic_update_slice.29
  456.3 3.5 dynamic_update_slice.30
  472.7 3.5 dynamic_update_slice.29
  476.2 3.5 dynamic_update_slice.30
  492.6 3.4 dynamic_update_slice.29
  496.0 3.4 dynamic_update_slice.30
  541.8 10.1 %all-to-all-start.3 = ((bf16[32,128,128]{1,2,0:T(8,128)(2,1)}), bf16[32,128,128]{1,2,0:T(8,128)(2,1)}, u32[]{:S(2)}, u32[]{:S(2)}) async-start(bf16[32,128,128]{1,2,0:T(8,128)(2,1)} %subtract_convert_fusion), calls=%async_computation.4 | async-start | bytes 2097152 | tf_op jit(solution)/shard_map/all_to_all | solution.py:264
  556.8 21.7 %all-to-all-done.3 = bf16[32,128,128]{1,2,0:T(8,128)(2,1)} async-done(((bf16[32,128,128]{1,2,0:T(8,128)(2,1)}), bf16[32,128,128]{1,2,0:T(8,128)(2,1)}, u32[]{:S(2)}, u32[]{:S(2)}) %all-to-all-start.3) | async-done | bytes 1048608 | tf_op jit(solution)/shard_map/all_to_all | solution.py:264
  578.5 5.6 all-to-all-start.4
  586.8 23.8 %all-to-all-done.4 = bf16[32,128,128]{2,1,0:T(8,128)(2,1)S(1)} async-done(((bf16[32,128,128]{2,1,0:T(8,128)(2,1)}), bf16[32,128,128]{2,1,0:T(8,128)(2,1)S(1)}, u32[]{:S(2)}, u32[]{:S(2)}) %all-to-all-start.4) | async-done | bytes 1048608 | tf_op jit(solution)/shard_map/all_to_all | solution.py:266
  610.6 5.4 all-to-all-start.5
  620.1 21.9 %all-to-all-done.5 = bf16[32,128,128]{2,1,0:T(8,128)(2,1)S(1)} async-done(((bf16[32,128,128]{2,1,0:T(8,128)(2,1)}), bf16[32,128,128]{2,1,0:T(8,128)(2,1)S(1)}, u32[]{:S(2)}, u32[]{:S(2)}) %all-to-all-start.5) | async-done | bytes 1048608 | tf_op jit(solution)/shard_map/all_to_all | solution.py:269
  (263 shorter events, 190.9 us)
Async XLA Ops:
  7.2 178.0 %copy-start = (bf16[64,128]{1,0:T(8,128)(2,1)S(1)}, bf16[64,128]{1,0:T(8,128)(2,1)}, u32[]{:S(2)}) copy-start(bf16[64,128]{1,0:T(8,128)(2,1)} %param.20) | copy-start | bytes 49156
  7.2 14.0 %copy-start.13 = (s32[1,128]{1,0:T(1,128)S(1)}, s32[1,128]{1,0:T(1,128)}, u32[]{:S(2)}) copy-start(s32[1,128]{1,0:T(1,128)} %param.19) | copy-start | bytes 1540
  7.2 14.3 %copy-start.12 = (s32[1,16]{1,0:T(1,128)S(1)}, s32[1,16]{1,0:T(1,128)}, u32[]{:S(2)}) copy-start(s32[1,16]{1,0:T(1,128)} %param.18) | copy-start | bytes 196
  7.2 15.5 %copy-start.6 = (bf16[1,128,1024]{2,1,0:T(8,128)(2,1)S(1)}, bf16[1,128,1024]{2,1,0:T(8,128)(2,1)}, u32[]{:S(2)}) copy-start(bf16[1,128,1024]{2,1,0:T(8,128)(2,1)} %param.14) | copy-start | bytes 786436
  9.5 13.3 %copy-start.7 = (bf16[1,128,1024]{2,1,0:T(8,128)(2,1)S(1)}, bf16[1,128,1024]{2,1,0:T(8,128)(2,1)}, u32[]{:S(2)}) copy-start(bf16[1,128,1024]{2,1,0:T(8,128)(2,1)} %param.15) | copy-start | bytes 786436
  9.5 39.7 %all-to-all-start.2 = ((bf16[128,32,128]{0,2,1:T(8,128)(2,1)}), bf16[128,32,128]{0,2,1:T(8,128)(2,1)S(1)}, u32[]{:S(2)}, u32[]{:S(2)}) async-start(bf16[128,32,128]{0,2,1:T(8,128)(2,1)} %bitcast.35), calls=%async_computation.2 | async-start | bytes 2097152 | tf_op jit(solution)/shard_map/all_to_all | solution.py:180
  50.5 32.5 %all-to-all-start.1 = ((bf16[128,32,128]{2,0,1:T(8,128)(2,1)}), bf16[128,32,128]{2,0,1:T(8,128)(2,1)S(1)}, u32[]{:S(2)}, u32[]{:S(2)}) async-start(bf16[128,32,128]{2,0,1:T(8,128)(2,1)} %bitcast.244), calls=%async_computation.1 | async-start | bytes 2097152 | tf_op jit(solution)/shard_map/all_to_all | solution.py:181
  83.0 10.6 %copy-start.2 = (bf16[128,32,128]{2,0,1:T(8,128)(2,1)}, bf16[128,32,128]{2,0,1:T(8,128)(2,1)S(1)}, u32[]{:S(2)}) copy-start(bf16[128,32,128]{2,0,1:T(8,128)(2,1)S(1)} %all-to-all-done.1) | copy-start | bytes 3145732
  84.3 32.2 %all-to-all-start = ((bf16[128,32,128]{2,0,1:T(8,128)(2,1)}), bf16[128,32,128]{2,0,1:T(8,128)(2,1)}, u32[]{:S(2)}, u32[]{:S(2)}) async-start(bf16[128,32,128]{2,0,1:T(8,128)(2,1)} %bitcast.245), calls=%async_computation | async-start | bytes 2097152 | tf_op jit(solution)/shard_map/all_to_all | solution.py:182
  90.0 268.9 %reduce-scatter.2.cloned.1.call-start = ((), (), s32[]{:S(2)}) async-start(), calls=%async_computation.7 | async-start | bytes 294912 | tf_op jit(solution)/shard_map/reduce_scatter | solution.py:235
  90.7 2.9 copy-start.10
  93.6 2.0 copy-start.4
  93.6 2.0 copy-start.11
  171.0 14.3 %copy-start.5 = (bf16[8,512,1,128]{1,3,2,0:T(8,128)(2,1)}, bf16[8,512,1,128]{1,3,2,0:T(8,128)(2,1)S(1)}, u32[]{:S(2)}) copy-start(bf16[8,512,1,128]{1,3,2,0:T(8,128)(2,1)S(1)} %get-tuple-element.121) | copy-start | bytes 3145732
  171.0 0.7 copy-start.9
  185.4 146.6 %copy-start.8 = (s32[4096]{0:T(1024)S(1)}, s32[4096]{0:T(1024)}, u32[]{:S(2)}) copy-start(s32[4096]{0:T(1024)} %get-tuple-element.214) | copy-start | bytes 49156
  541.8 10.1 %copy-start.1 = (f32[4096,128]{1,0:T(8,128)S(1)}, f32[4096,128]{1,0:T(8,128)}, u32[]{:S(2)}) copy-start(f32[4096,128]{1,0:T(8,128)} %get-tuple-element.124) | copy-start | bytes 6291460
  541.8 36.7 %all-to-all-start.3 = ((bf16[32,128,128]{1,2,0:T(8,128)(2,1)}), bf16[32,128,128]{1,2,0:T(8,128)(2,1)}, u32[]{:S(2)}, u32[]{:S(2)}) async-start(bf16[32,128,128]{1,2,0:T(8,128)(2,1)} %subtract_convert_fusion), calls=%async_computation.4 | async-start | bytes 2097152 | tf_op jit(solution)/shard_map/all_to_all | solution.py:264
  551.9 2.0 copy-start.3
  578.5 32.1 %all-to-all-start.4 = ((bf16[32,128,128]{2,1,0:T(8,128)(2,1)}), bf16[32,128,128]{2,1,0:T(8,128)(2,1)S(1)}, u32[]{:S(2)}, u32[]{:S(2)}) async-start(bf16[32,128,128]{2,1,0:T(8,128)(2,1)} %bitcast.243), calls=%async_computation.5 | async-start | bytes 2097152 | tf_op jit(solution)/shard_map/all_to_all | solution.py:266
  610.6 31.4 %all-to-all-start.5 = ((bf16[32,128,128]{2,1,0:T(8,128)(2,1)}), bf16[32,128,128]{2,1,0:T(8,128)(2,1)S(1)}, u32[]{:S(2)}, u32[]{:S(2)}) async-start(bf16[32,128,128]{2,1,0:T(8,128)(2,1)} %bitcast.60), calls=%async_computation.6 | async-start | bytes 2097152 | tf_op jit(solution)/shard_map/all_to_all | solution.py:269
Sparse Core Ops, SparseCore 0:
  332.0 26.8 reduce-scatter.1
where the time goes:
time: 659 us; the launch traced here: 650 us
  waiting for transfers between devices  162 us (25%)
  blocking collectives  153 us (23%)
  local copies, waits for them, and re-layouts  123 us (19%)
  matrix products  98.8 us (15%)
  starting transfers between devices  44 us (7%)
  other arithmetic  33.7 us (5%)
  loops' own time  21.5 us (3%)
  between operations  14.5 us (2%)
    psum x1, blocking collectives, on_device(): similarity_pool = lax.psum(running_mixture_vector, 'seq') / softmax_divisor  140 us
    dot_general x16, matrix products, one_block(): jnp.einsum('qhd,kd->hqk', query_block, key_block, preferred_element_type=...  31.9 us
    dynamic_update_slice x8, local copies, waits for them, and re-layouts, one_block(): lax.dynamic_update_slice_in_dim(key_total, lax.dynamic_slice_in_dim(key_t...  26.9 us
    dynamic_update_slice x8, local copies, waits for them, and re-layouts, one_block(): lax.dynamic_update_slice_in_dim(value_total, lax.dynamic_slice_in_dim(val...  26.8 us
    all_to_all x1, waiting for transfers between devices, on_device(): lax.all_to_all(queries[0], 'seq', split_axis=1, concat_axis=0, tiled=True)  26.3 us
    reduce_scatter x1, waiting for transfers between devices, on_device(): lax.psum_scatter(lax.dot_general(dense, query_float, (((0,), (0,)), ((),...  25.4 us
    all_to_all x1, waiting for transfers between devices, on_device(): lax.all_to_all(key_local.astype(jnp.bfloat16), 'seq', split_axis=0, conca...  23.8 us
    all_to_all x1, waiting for transfers between devices, on_device(): lax.all_to_all(repeated_keys, 'seq', split_axis=1, concat_axis=0, tiled=T...  23.7 us
  transfers between devices with their start and end apart: 7, of which 7 were waited for; matrix products, arithmetic and copies ran while one was open for 4% of the time, Pallas kernels for 0%

commit v1 on v0

v1 whole, which is shorter than its diff:
```python
import functools
import math

import jax
import jax.numpy as jnp
from jax import lax
from jax.experimental import pallas as pl
from jax.experimental.pallas import tpu as pltpu
from jax.sharding import PartitionSpec as P

WIDTH = 128
NY = 4
NZ = 8
NPB = 8
BLOCK = 128
ROWS = 512
WINDOW = 1152
CHUNK = 384
SPANS = 128
QUERIES = 512
CAND = 8
EPS = 1e-06
MASKED = 16384.0
LOG2E = math.log2(math.e)
SCALE = 1.0 / math.sqrt(WIDTH)
F32 = jnp.float32
BF16 = jnp.bfloat16
MESH = pl.DeviceIdType.MESH
NT = (((1,), (1,)), ((), ()))


def dot(a, b):
    return jnp.dot(a, b, preferred_element_type=F32)


def dot_nt(a, b):
    return lax.dot_general(a, b, NT, preferred_element_type=F32)


def iota(shape, dim):
    return lax.broadcasted_iota(jnp.int32, shape, dim)


def aligned(start, size, unit=128):
    return pl.ds(pl.multiple_of(start, unit), size)


def column(row):
    return jnp.transpose(jnp.broadcast_to(row, (128, 128)))


def segments(lens):
    down = column(lens)
    across = jnp.broadcast_to(lens, (128, 128))
    sub, lane = iota((128, 128), 0), iota((128, 128), 1)
    first_row = jnp.sum(jnp.where(sub < lane, down, 0.0), axis=0, keepdims=True)
    first_col = jnp.sum(jnp.where(lane < sub, across, 0.0), axis=1, keepdims=True)
    return first_row, first_row + lens, first_col, first_col + down[:, :1]


def body(
    q_ref, k_ref, v_ref, e_ref, qgain_ref, kgain_ref, dlen_ref, slen_ref, ans_ref,
    loss_ref, gq_ref, gk_ref, gv_ref,
    qraw, kraw, vraw, qe, ka, kt, va, vt, qst, qraw_t, qrec, w, ot, ef, sp, sgt, doa, dss, dk, dv,
    dqb, dkb, dvb, hsend, hrecv, hot_c, hot_t, rsb, zb, pbb, agb, mysc,
    kv_s, kv_r, q_s, q_r, h_s, h_r, e_s, e_r, x_s, x_r, c_s, c_r, loc,
    rs_s, rs_r, z_s, z_r, p_s, p_r, a_s, a_r,
    gq_s, gq_r, bh_s, bh_r, bk_s, bk_r,
):
    me = lax.axis_index("seq")
    pb = lax.axis_index("pb")
    z = me // NY
    y = me % NY
    up = (z + 1) % NZ
    down = (z + NZ - 1) % NZ
    sibling = pb + 1 - 2 * (pb % 2)

    def at(zz, yy):
        return {"seq": zz * NY + yy, "pb": pb}

    def remote(src, dst, ss, rs, dev):
        return pltpu.make_async_remote_copy(
            src_ref=src, dst_ref=dst, send_sem=ss, recv_sem=rs, device_id=dev, device_id_type=MESH
        )

    barrier = pltpu.get_barrier_semaphore()

    def greet(dev):
        pl.semaphore_signal(barrier, inc=1, device_id=dev, device_id_type=MESH)

    for k in range(1, NY):
        greet(at(z, (y + k) % NY))
    for k in range(1, NZ):
        greet(at((z + k) % NZ, y))
    for k in range(1, NPB):
        greet({"seq": me, "pb": (pb + k) % NPB})
    for zi in range(2):
        for yi in range(NY):
            source_z = 2 * y + zi

            @pl.when(jnp.logical_or(source_z != z, yi != y))
            def _():
                greet(at(source_z, yi))

    e_yy = z // 2
    e_self = (e_yy == y).astype(jnp.int32)
    pl.semaphore_wait(barrier, (NY - 1) + (NZ - 1) + (NPB - 1) + NZ - e_self)

    def kv_copy(dy, g, which):
        src, dst = (k_ref, kraw) if which == 0 else (v_ref, vraw)
        ty = (y + dy) % NY
        return remote(
            src.at[:, aligned(ty * 256 + g * 128, 128)],
            dst.at[aligned(ROWS + y * BLOCK, BLOCK), pl.ds(g * 128, 128)],
            kv_s.at[dy - 1, g, which],
            kv_r.at[dy - 1, g, which],
            at(z, ty),
        )

    def kv_landed(dy, g, which):
        src, dst = (k_ref, kraw) if which == 0 else (v_ref, vraw)
        sy = (y + NY - dy) % NY
        return remote(
            src.at[:, aligned(y * 256 + g * 128, 128)],
            dst.at[aligned(ROWS + sy * BLOCK, BLOCK), pl.ds(g * 128, 128)],
            kv_s.at[dy - 1, g, which],
            kv_r.at[dy - 1, g, which],
            at(z, sy),
        )

    def q_copy(dy, g):
        ty = (y + dy) % NY
        return remote(
            q_ref.at[:, aligned(ty * 1024 + g * 512, 512)],
            qraw.at[aligned(y * BLOCK, BLOCK), aligned(g * 512, 512)],
            q_s.at[dy - 1, g],
            q_r.at[dy - 1, g],
            at(z, ty),
        )

    def q_landed(dy, g):
        sy = (y + NY - dy) % NY
        return remote(
            q_ref.at[:, aligned(y * 1024 + g * 512, 512)],
            qraw.at[aligned(sy * BLOCK, BLOCK), aligned(g * 512, 512)],
            q_s.at[dy - 1, g],
            q_r.at[dy - 1, g],
            at(z, sy),
        )

    own_rows = aligned(ROWS + y * BLOCK, BLOCK)
    local = [
        pltpu.make_async_copy(k_ref.at[:, aligned(y * 256, 256)], kraw.at[own_rows, :], loc.at[0]),
        pltpu.make_async_copy(v_ref.at[:, aligned(y * 256, 256)], vraw.at[own_rows, :], loc.at[1]),
        pltpu.make_async_copy(
            q_ref.at[:, aligned(y * 1024, 1024)], qraw.at[aligned(y * BLOCK, BLOCK), :], loc.at[2]
        ),
        pltpu.make_async_copy(
            e_ref, qe.at[pb, :, aligned((z % 2) * 512 + y * 128, 128)], loc.at[3]
        ),
    ]
    local[0].start()
    local[1].start()
    order = (2, 1, 3)
    for g in range(2):
        for which in range(2):
            for dy in order:
                kv_copy(dy, g, which).start()
    local[2].start()

    def e_copy(k):
        tz = (z + k) % NZ
        col = aligned((z % 2) * 512 + y * 128, 128)
        return remote(e_ref, qe.at[pb, :, col], e_s.at[k], e_r.at[z % 2, y], at(tz, e_yy))

    @pl.when(e_self == 1)
    def _():
        local[3].start()

    for k in range(NZ):
        if k == 0:

            @pl.when(e_self == 0)
            def _():
                e_copy(0).start()
        else:
            e_copy(k).start()

    for g in range(2):
        for dy in order:
            q_copy(dy, g).start()

    dfirst_r, dend_r, dfirst_c, dend_c = segments(dlen_ref[...])
    sfirst_r, send_r, sfirst_c, send_c = segments(slen_ref[...])
    span_col = column(slen_ref[...])[:, :1]
    qgain_col = column(qgain_ref[...])[:, :1]
    kgain = kgain_ref[...]
    base = z * ROWS
    tok_c = (base + iota((SPANS, ROWS), 1)).astype(F32)
    hot_c[...] = jnp.where(
        jnp.logical_and(tok_c >= sfirst_c, tok_c < send_c), 1.0, 0.0
    ).astype(BF16)
    tok_k = base - ROWS + iota((3 * ROWS, 128), 0)
    tok_kf = tok_k.astype(F32)
    lane_k = iota((3 * ROWS, 128), 1)
    same = jnp.logical_and(tok_kf >= dfirst_r, tok_kf < dend_r)
    outside = jnp.logical_and(
        lane_k == 127, jnp.logical_or(tok_k < 0, tok_k >= NZ * ROWS)
    )
    kdoc = jnp.where(jnp.logical_or(same, outside), 1.0, 0.0).astype(BF16)
    ones_v = jnp.where(lane_k < 3, 1.0, 0.0).astype(BF16)
    for g in range(2):
        ka[g, :, 128:256] = kdoc
        va[g, :, 128:256] = ones_v
    tok_q = (base + iota((128, ROWS), 1)).astype(F32)
    hot_t[...] = jnp.where(
        jnp.logical_and(tok_q >= dfirst_c, tok_q < dend_c), 0.0, -MASKED
    ).astype(BF16)
    sp[...] = jnp.zeros_like(sp)

    def halo(b, g, which, direction):
        buf = kraw if which == 0 else vraw
        cols = pl.ds(g * 128, 128)
        dst_row = b * BLOCK + (0 if direction == 0 else 2 * ROWS)
        return remote(
            buf.at[aligned(ROWS + b * BLOCK, BLOCK), cols],
            buf.at[aligned(dst_row, BLOCK), cols],
            h_s.at[b, g, which, direction],
            h_r.at[b, g, which, direction],
            at(up if direction == 0 else down, y),
        )

    local[0].wait()
    local[1].wait()
    for g in range(2):
        for which in range(2):
            for direction in range(2):
                halo(y, g, which, direction).start()
        for dy in (1, 3, 2):
            for which in range(2):
                kv_landed(dy, g, which).wait_recv()
                for direction in range(2):
                    halo((y + NY - dy) % NY, g, which, direction).start()

    @pl.when(e_self == 1)
    def _():
        local[3].wait()

    for zi in range(2):
        for yi in range(NY):

            @pl.when(jnp.logical_or(2 * y + zi != z, yi != y))
            def _():
                remote(
                    e_ref, qe.at[pb, :, pl.ds(zi * 512 + yi * 128, 128)], e_s.at[0],
                    e_r.at[zi, yi], at(2 * y + zi, yi),
                ).wait_recv()

    def x_copy(k):
        return remote(
            qe.at[pb], qe.at[pb], x_s.at[k - 1], x_r.at[k - 1],
            {"seq": me, "pb": (pb + 2 * k) % NPB},
        )

    def x_landed(k):
        src = (pb + NPB - 2 * k) % NPB
        return remote(
            qe.at[src], qe.at[src], x_s.at[k - 1], x_r.at[k - 1], {"seq": me, "pb": src}
        )

    def c_copy(k):
        part = (pb + NPB - 2 * k) % NPB
        return remote(
            qe.at[part], qe.at[part], c_s.at[k], c_r.at[k], {"seq": me, "pb": sibling}
        )

    def c_landed(k):
        part = (sibling + NPB - 2 * k) % NPB
        return remote(
            qe.at[part], qe.at[part], c_s.at[k], c_r.at[k], {"seq": me, "pb": sibling}
        )

    for k in (2, 1, 3):
        x_copy(k).start()
    c_copy(0).start()

    local[2].wait()
    def forward_group(g, _):
        for b in range(NY):
            for which in range(2):
                for direction in range(2):
                    halo(b, g, which, direction).wait_recv()
        cols = aligned(g * 128, 128)
        key = kraw[:, cols].astype(F32)
        rec = lax.rsqrt(jnp.mean(key * key, axis=1, keepdims=True) + EPS)
        key = key * rec * kgain
        ka[g, :, 0:128] = key.astype(BF16)
        kt[g] = jnp.transpose(key).astype(BF16)
        val = vraw[:, cols]
        va[g, :, 0:128] = val
        vt[g] = jnp.transpose(val.astype(F32)).astype(BF16)

        def tile(i, _):
            r = (y + i) % NY

            @pl.when(i != 0)
            def _():
                q_landed(NY - i, g).wait_recv()

            idx = g * NY + r
            rows = aligned(r * BLOCK, BLOCK)
            x = qraw[rows, aligned(g * 512, 512)].astype(F32)
            x = jnp.concatenate(
                [jnp.transpose(x[:, h * 128 : (h + 1) * 128]) for h in range(4)], axis=1
            )
            qraw_t[idx] = x.astype(BF16)
            rq = lax.rsqrt(jnp.mean(x * x, axis=0, keepdims=True) + EPS)
            qrec[idx] = rq
            qst[idx, 0:128, :] = (x * rq * qgain_col).astype(BF16)
            qdoc = hot_t[:, rows]
            qst[idx, 128:256, :] = jnp.concatenate([qdoc] * 4, axis=1)
            rhs = qst[idx]
            total = jnp.zeros((1, 512), F32)
            for c in range(WINDOW // CHUNK):
                part = slice(c * CHUNK, (c + 1) * CHUNK)
                s = dot(ka[g, aligned(r * BLOCK + c * CHUNK, CHUNK), :], rhs)
                e = jnp.exp2(s * (LOG2E * SCALE))
                total = total + jnp.sum(e, axis=0, keepdims=True)
                ef[part, :] = e
            inv = 1.0 / total
            for c in range(WINDOW // CHUNK):
                part = slice(c * CHUNK, (c + 1) * CHUNK)
                w[idx, part, :] = (ef[part, :] * inv).astype(BF16)
            out = dot(vt[g, :, aligned(r * BLOCK, WINDOW)], w[idx]).astype(BF16)
            ot[idx] = out
            table = hot_c[:, rows]
            for h in range(4):
                hc = aligned(g * 512 + h * 128, 128)
                sp[:, hc] += dot_nt(table, out[:, h * 128 : (h + 1) * 128])
            return 0

        lax.fori_loop(0, NY, tile, 0)
        return 0

    lax.fori_loop(0, 2, forward_group, 0)

    for k in range(1, 4):
        x_landed(k).wait_recv()
        c_copy(k).start()
    for k in range(4):
        c_landed(k).wait_recv()

    emb = qe[...].reshape(QUERIES, 1024)
    span = (sp[...] / span_col).astype(BF16)
    sims = dot_nt(span, emb)
    mine = ans_ref[...] - pb * SPANS
    span_no = iota((SPANS, QUERIES), 0)
    for j in range(CAND):
        mysc[j : j + 1, :] = jnp.sum(
            jnp.where(span_no == mine[j : j + 1, :], sims, 0.0), axis=0, keepdims=True
        )

    def lanes(t):
        return aligned(t * 128, 128)

    def rs_copy(dy):
        ty = (y + dy) % NY
        return remote(mysc.at[:, lanes(ty)], rsb.at[y], rs_s.at[dy - 1], rs_r.at[dy - 1], at(z, ty))

    def rs_landed(dy):
        sy = (y + NY - dy) % NY
        return remote(mysc.at[:, lanes(y)], rsb.at[sy], rs_s.at[dy - 1], rs_r.at[dy - 1], at(z, sy))

    def z_copy(k):
        return remote(zb.at[z], zb.at[z], z_s.at[k - 1], z_r.at[k - 1], at((z + k) % NZ, y))

    def z_landed(k):
        src = (z + NZ - k) % NZ
        return remote(zb.at[src], zb.at[src], z_s.at[k - 1], z_r.at[k - 1], at(src, y))

    def p_copy(k):
        return remote(
            pbb.at[pb], pbb.at[pb], p_s.at[k - 1], p_r.at[k - 1],
            {"seq": me, "pb": (pb + k) % NPB},
        )

    def p_landed(k):
        src = (pb + NPB - k) % NPB
        return remote(
            pbb.at[src], pbb.at[src], p_s.at[k - 1], p_r.at[k - 1], {"seq": me, "pb": src}
        )

    def a_copy(dy):
        ty = (y + dy) % NY
        return remote(agb.at[y], agb.at[y], a_s.at[dy - 1], a_r.at[dy - 1], at(z, ty))

    def a_landed(dy):
        sy = (y + NY - dy) % NY
        return remote(agb.at[sy], agb.at[sy], a_s.at[dy - 1], a_r.at[dy - 1], at(z, sy))

    for dy in order:
        rs_copy(dy).start()
    rsb[y] = mysc[:, lanes(y)]
    for dy in order:
        rs_landed(dy).wait_recv()
    part = rsb[0]
    for t in range(1, NY):
        part = part + rsb[t]
    zb[z] = part
    for k in (4, 3, 5, 2, 6, 1, 7):
        z_copy(k).start()
    for k in range(1, NZ):
        z_landed(k).wait_recv()
    part = zb[0]
    for t in range(1, NZ):
        part = part + zb[t]
    pbb[pb] = part
    for k in (4, 3, 5, 2, 6, 1, 7):
        p_copy(k).start()
    for k in range(1, NPB):
        p_landed(k).wait_recv()
    part = pbb[0]
    for t in range(1, NPB):
        part = part + pbb[t]
    agb[y] = part
    for dy in order:
        a_copy(dy).start()
    for dy in order:
        a_landed(dy).wait_recv()
    sims = jnp.concatenate([agb[t] for t in range(NY)], axis=1) / 0.05
    ex = jnp.exp(sims)
    den = jnp.sum(ex, axis=0, keepdims=True)
    loss = jnp.log(den) - sims[0:1, :]
    own_loss = jnp.zeros((1, QUERIES // NPB), F32)
    for t in range(NPB):
        size = QUERIES // NPB
        own_loss = jnp.where(pb == t, loss[:, t * size : (t + 1) * size], own_loss)
    loss_ref[...] = own_loss
    hit = (iota((CAND, QUERIES), 0) == 0).astype(F32)
    weight = 256.0 * (ex / den - hit) / 0.05
    dense = jnp.zeros((SPANS, QUERIES), F32)
    for j in range(CAND):
        dense = dense + jnp.where(span_no == mine[j : j + 1, :], weight[j : j + 1, :], 0.0)
    high = dense.astype(BF16)
    low = (dense - high.astype(F32)).astype(BF16)
    sg = (dot(high, emb) + dot(low, emb)) / span_col
    for h in range(8):
        cols = slice(h * 128, (h + 1) * 128)
        sgt[cols, :] = jnp.transpose(sg[:, cols]).astype(BF16)

    def gq_copy(g, r, slot):
        return remote(
            dqb.at[aligned(r * BLOCK, BLOCK), aligned(g * 512, 512)],
            gq_ref.at[:, aligned(y * 1024 + g * 512, 512)],
            gq_s.at[slot, g],
            gq_r.at[slot, g],
            at(z, r),
        )

    def gq_landed(g, r, slot):
        return remote(
            dqb.at[aligned(r * BLOCK, BLOCK), aligned(g * 512, 512)],
            gq_ref.at[:, aligned(r * 1024 + g * 512, 512)],
            gq_s.at[slot, g],
            gq_r.at[slot, g],
            at(z, r),
        )

    def gq_local(g):
        return pltpu.make_async_copy(
            dqb.at[aligned(y * BLOCK, BLOCK), aligned(g * 512, 512)],
            gq_ref.at[:, aligned(y * 1024 + g * 512, 512)],
            loc.at[4 + g],
        )

    def back_halo(g, which, direction):
        return remote(
            hsend.at[direction, g, which],
            hrecv.at[direction, g, which],
            bh_s.at[direction, g, which],
            bh_r.at[direction, g, which],
            at(down if direction == 0 else up, y),
        )

    def backward_group(g, _):
        dk[g] = jnp.zeros((3 * ROWS, 128), F32)
        dv[g] = jnp.zeros((3 * ROWS, 128), F32)

        def tile(i, _):
            off = jnp.where(i == 0, 2, jnp.where(i == 1, 1, jnp.where(i == 2, 3, 0)))
            r = (y + off) % NY
            idx = g * NY + r
            rows = aligned(r * BLOCK, BLOCK)
            go = dot(sgt[aligned(g * 512, 512), :], hot_c[:, rows])
            go = jnp.concatenate([go[h * 128 : (h + 1) * 128, :] for h in range(4)], axis=1)
            gob = go.astype(BF16)
            delta = jnp.sum(go * ot[idx].astype(F32), axis=0, keepdims=True)
            d0 = delta.astype(BF16).astype(F32)
            d1 = (delta - d0).astype(BF16).astype(F32)
            d2 = delta - d0 - d1
            row = iota((128, 512), 0)
            extra = jnp.where(row == 0, -d0, jnp.where(row == 1, -d1, jnp.where(row == 2, -d2, 0.0)))
            doa[0:128, :] = gob
            doa[128:256, :] = extra.astype(BF16)
            rhs = doa[...]
            for c in range(WINDOW // CHUNK):
                dp = dot(va[g, aligned(r * BLOCK + c * CHUNK, CHUNK), :], rhs)
                part = slice(c * CHUNK, (c + 1) * CHUNK)
                dss[part, :] = (w[idx, part, :].astype(F32) * dp).astype(BF16)
            window = aligned(r * BLOCK, WINDOW)
            dv[g, window, :] += dot_nt(w[idx], gob)
            dk[g, window, :] += dot_nt(dss[...], qst[idx, 0:128, :])
            dq = dot(kt[g, :, window], dss[...])
            x = qraw_t[idx].astype(F32)
            rq = qrec[idx]
            gained = (qgain_col * SCALE) * dq
            mean = jnp.mean(x * gained, axis=0, keepdims=True)
            res = rq * gained - x * (rq * rq * rq * mean)
            for h in range(4):
                dqb[rows, aligned(g * 512 + h * 128, 128)] = jnp.transpose(
                    res[:, h * 128 : (h + 1) * 128]
                ).astype(BF16)

            @pl.when(i != 3)
            def _():
                gq_copy(g, r, i).start()

            @pl.when(i == 3)
            def _():
                gq_local(g).start()

            return 0

        lax.fori_loop(0, NY, tile, 0)
        hsend[0, g, 0] = (dk[g, 0:ROWS, :] * SCALE).astype(BF16)
        hsend[0, g, 1] = dv[g, 0:ROWS, :].astype(BF16)
        hsend[1, g, 0] = (dk[g, 2 * ROWS : 3 * ROWS, :] * SCALE).astype(BF16)
        hsend[1, g, 1] = dv[g, 2 * ROWS : 3 * ROWS, :].astype(BF16)
        for which in range(2):
            for direction in range(2):
                back_halo(g, which, direction).start()
        return 0

    lax.fori_loop(0, 2, backward_group, 0)

    def bk_copy(dy, g, which):
        ty = (y + dy) % NY
        src, dst = (dkb, gk_ref) if which == 0 else (dvb, gv_ref)
        return remote(
            src.at[aligned(ty * BLOCK, BLOCK), pl.ds(g * 128, 128)],
            dst.at[:, aligned(y * 256 + g * 128, 128)],
            bk_s.at[dy - 1, g, which],
            bk_r.at[dy - 1, g, which],
            at(z, ty),
        )

    def bk_landed(dy, g, which):
        sy = (y + NY - dy) % NY
        src, dst = (dkb, gk_ref) if which == 0 else (dvb, gv_ref)
        return remote(
            src.at[aligned(sy * BLOCK, BLOCK), pl.ds(g * 128, 128)],
            dst.at[:, aligned(sy * 256 + g * 128, 128)],
            bk_s.at[dy - 1, g, which],
            bk_r.at[dy - 1, g, which],
            at(z, sy),
        )

    def bk_local(g, which):
        src, dst = (dkb, gk_ref) if which == 0 else (dvb, gv_ref)
        return pltpu.make_async_copy(
            src.at[aligned(y * BLOCK, BLOCK), pl.ds(g * 128, 128)],
            dst.at[:, aligned(y * 256 + g * 128, 128)],
            loc.at[6 + 2 * g + which],
        )

    for g in range(2):
        cols = slice(g * 128, (g + 1) * 128)
        for direction in range(2):
            for which in range(2):
                back_halo(g, which, direction).wait_recv()
        vtot = dv[g, ROWS : 2 * ROWS, :] + hrecv[0, g, 1].astype(F32) + hrecv[1, g, 1].astype(F32)
        dvb[:, cols] = vtot.astype(BF16)
        for dy in order:
            bk_copy(dy, g, 1).start()
        bk_local(g, 1).start()
        ktot = (
            dk[g, ROWS : 2 * ROWS, :] * SCALE
            + hrecv[0, g, 0].astype(F32)
            + hrecv[1, g, 0].astype(F32)
        )
        x = kraw[ROWS : 2 * ROWS, cols].astype(F32)
        rec = lax.rsqrt(jnp.mean(x * x, axis=1, keepdims=True) + EPS)
        gained = kgain * ktot
        mean = jnp.mean(x * gained, axis=1, keepdims=True)
        dkb[:, cols] = (rec * gained - x * (rec * rec * rec * mean)).astype(BF16)
        for dy in order:
            bk_copy(dy, g, 0).start()
        bk_local(g, 0).start()

    for g in range(2):
        gq_local(g).wait()
        for slot, off in enumerate((2, 1, 3)):
            gq_copy(g, (y + off) % NY, slot).wait_send()
            gq_landed(g, (y + NY - off) % NY, slot).wait_recv()
            q_copy(off, g).wait_send()
        for which in range(2):
            bk_local(g, which).wait()
            for dy in order:
                bk_copy(dy, g, which).wait_send()
                bk_landed(dy, g, which).wait_recv()
                kv_copy(dy, g, which).wait_send()
            for direction in range(2):
                back_halo(g, which, direction).wait_send()
                for b in range(NY):
                    halo(b, g, which, direction).wait_send()
    for dy in order:
        rs_copy(dy).wait_send()
        a_copy(dy).wait_send()
        x_copy(dy).wait_send()
    for k in range(4):
        c_copy(k).wait_send()
    for k in range(1, NZ):
        z_copy(k).wait_send()
        p_copy(k).wait_send()
        e_copy(k).wait_send()

    @pl.when(e_self == 0)
    def _():
        e_copy(0).wait_send()


def on_device(
    queries, keys, values, query_gain, key_gain, doc_lengths, span_lengths, query_emb, answer_options
):
    dlen = jnp.pad(doc_lengths.astype(F32), ((0, 0), (0, 128 - doc_lengths.shape[1])))
    slen = span_lengths.astype(F32)
    anywhere = pl.BlockSpec(memory_space=pl.ANY)
    vmem = pl.BlockSpec(memory_space=pltpu.VMEM)

    def dma(*shape):
        return pltpu.SemaphoreType.DMA(shape)

    tok = BLOCK
    loss, gq, gk, gv = pl.pallas_call(
        body,
        out_shape=(
            jax.ShapeDtypeStruct((1, QUERIES // NPB), F32),
            jax.ShapeDtypeStruct((tok, 4096), BF16),
            jax.ShapeDtypeStruct((tok, 1024), BF16),
            jax.ShapeDtypeStruct((tok, 1024), BF16),
        ),
        in_specs=[anywhere] * 4 + [vmem] * 5,
        out_specs=(vmem, anywhere, anywhere, anywhere),
        scratch_shapes=[
            pltpu.VMEM((ROWS, 1024), BF16),
            pltpu.VMEM((3 * ROWS, 256), BF16),
            pltpu.VMEM((3 * ROWS, 256), BF16),
            pltpu.VMEM((NPB, QUERIES // NPB, 1024), BF16),
            pltpu.VMEM((2, 3 * ROWS, 256), BF16),
            pltpu.VMEM((2, 128, 3 * ROWS), BF16),
            pltpu.VMEM((2, 3 * ROWS, 256), BF16),
            pltpu.VMEM((2, 128, 3 * ROWS), BF16),
            pltpu.VMEM((8, 256, 512), BF16),
            pltpu.VMEM((8, 128, 512), BF16),
            pltpu.VMEM((8, 1, 512), F32),
            pltpu.VMEM((8, WINDOW, 512), BF16),
            pltpu.VMEM((8, 128, 512), BF16),
            pltpu.VMEM((WINDOW, 512), F32),
            pltpu.VMEM((SPANS, 1024), F32),
            pltpu.VMEM((1024, SPANS), BF16),
            pltpu.VMEM((256, 512), BF16),
            pltpu.VMEM((WINDOW, 512), BF16),
            pltpu.VMEM((2, 3 * ROWS, 128), F32),
            pltpu.VMEM((2, 3 * ROWS, 128), F32),
            pltpu.VMEM((ROWS, 1024), BF16),
            pltpu.VMEM((ROWS, 256), BF16),
            pltpu.VMEM((ROWS, 256), BF16),
            pltpu.VMEM((2, 2, 2, ROWS, 128), BF16),
            pltpu.VMEM((2, 2, 2, ROWS, 128), BF16),
            pltpu.VMEM((SPANS, ROWS), BF16),
            pltpu.VMEM((128, ROWS), BF16),
            pltpu.VMEM((NY, 8, 128), F32),
            pltpu.VMEM((NZ, 8, 128), F32),
            pltpu.VMEM((NPB, 8, 128), F32),
            pltpu.VMEM((NY, 8, 128), F32),
            pltpu.VMEM((CAND, QUERIES), F32),
            dma(3, 2, 2), dma(3, 2, 2),
            dma(3, 2), dma(3, 2),
            dma(NY, 2, 2, 2), dma(NY, 2, 2, 2),
            dma(NZ), dma(2, NY),
            dma(3), dma(3),
            dma(4), dma(4),
            dma(10),
            dma(3), dma(3),
            dma(7), dma(7),
            dma(7), dma(7),
            dma(3), dma(3),
            dma(3, 2), dma(3, 2),
            dma(2, 2, 2), dma(2, 2, 2),
            dma(3, 2, 2), dma(3, 2, 2),
        ],
        compiler_params=pltpu.CompilerParams(
            collective_id=0, has_side_effects=True, vmem_limit_bytes=56 * 1024 * 1024
        ),
        cost_estimate=pl.CostEstimate(
            flops=8 * 6 * 2 * WINDOW * 512 * 128, bytes_accessed=3 << 20, transcendentals=8 * WINDOW * 512
        ),
        name="attention_contrastive",
    )(
        queries[0],
        keys[0],
        values[0],
        query_emb,
        query_gain.reshape(1, 128),
        key_gain.reshape(1, 128),
        dlen,
        slen,
        answer_options.T,
    )
    return loss.reshape(QUERIES // NPB), gq[None], gk[None], gv[None]


def solution(mesh):
    in_specs = (
        P("pb", "seq", None),
        P("pb", "seq", None),
        P("pb", "seq", None),
        P(),
        P(),
        P("pb", None),
        P("pb", None),
        P("pb", "seq"),
        P(),
    )
    out_specs = (P("pb"), P("pb", "seq", None), P("pb", "seq", None), P("pb", "seq", None))
    return jax.shard_map(
        on_device, mesh=mesh, in_specs=in_specs, out_specs=out_specs, check_vma=False
    )
```

time: 659 us -> 89.6 us (0.14); the launches traced: 650 us -> 89.4 us
  waiting for transfers between devices: 162 us -> 0 us
  blocking collectives: 153 us -> 0 us
  local copies, waits for them, and re-layouts: 123 us -> 6.51 us
  matrix products: 98.8 us -> 0 us
  Pallas kernels: 0 us -> 81.7 us
  starting transfers between devices: 44 us -> 0 us
  other arithmetic: 33.7 us -> 0.51 us
  loops' own time: 21.5 us -> 0 us
  between operations: 14.5 us -> 0.66 us
    psum x1 -> x0, blocking collectives: 140 us -> none  [on_device(): similarity_pool = lax.psum(running_mixture_vector, 'seq') / softmax_divisor]
    all_to_all x6 -> x0, waiting for transfers between devices: 137 us -> none  [the longest x1 26.3 us: on_device(): lax.all_to_all(queries[0], 'seq', split_axis=1, concat_axis=0, tiled=True)]
    dot_general x59 -> x0, matrix products: 98.8 us -> none  [the longest x16 31.9 us: one_block(): jnp.einsum('qhd,kd->hqk', query_block, key_block, preferred_element_type=...]
    pallas_call x0 -> x1, Pallas kernels: none -> 81.7 us  [on_device(): pl.pallas_call(body, out_shape=(jax.ShapeDtypeStruct((1, QUERIES // NPB),...]
    dynamic_update_slice x40 -> x0, local copies, waits for them, and re-layouts: 65.2 us -> none  [the longest x8 26.9 us: one_block(): lax.dynamic_update_slice_in_dim(key_total, lax.dynamic_slice_in_dim(key_t...]
    all_to_all x6 -> x0, starting transfers between devices: 44 us -> none  [the longest x1 11.6 us: on_device(): lax.all_to_all(queries[0], 'seq', split_axis=1, concat_axis=0, tiled=True)]
    reduce_scatter x1 -> x0, waiting for transfers between devices: 25.4 us -> none  [on_device(): lax.psum_scatter(lax.dot_general(dense, query_float, (((0,), (0,)), ((),...]
    another operation x2 -> x0, loops' own time: 21.5 us -> none  [the longest x1 11.1 us: attend_backward(): lax.scan(one_block, (empty, empty), jnp.arange(length // rows, dtype=jnp....]
  transfers between devices with their start and end apart: 7 -> 0, of which waited for: 7 -> 0; matrix products, arithmetic and copies ran while one was open for 4% -> 0% of each run, Pallas kernels for 0% -> 0%
where the time goes in v1:
time: 89.6 us; the launch traced here: 89.4 us
  Pallas kernels  81.7 us (91%)
  local copies, waits for them, and re-layouts  6.51 us (7%)
    pallas_call x1, Pallas kernels, on_device(): pl.pallas_call(body, out_shape=(jax.ShapeDtypeStruct((1, QUERIES // NPB),...  81.7 us
    unnamed x14, local copies, waits for them, and re-layouts  5.99 us

profile of v1, /device:TPU:2, one launch (start us, length us, event | category | flops | bytes accessed | tf_op | source)
XLA Modules:
  0.0 89.4 jit_solution(13372391943409593131)
XLA Ops:
  0.6 0.0 copy-start.2
  0.6 0.6 copy-done.2
  1.3 0.0 copy-start.3
  1.3 0.5 pad.4.dlen_ref
  1.8 0.1 copy-done.3
  1.9 0.5 convert_element_type.9.slen_ref
  2.5 81.7 %attention_contrastive.1 = (f32[1,64]{1,0:T(1,128)}, bf16[128,4096]{1,0:T(8,128)(2,1)}, bf16[128,1024]{1,0:T(8,128)(2,1)}, bf16[128,1024]{1,0:T(8,128)(2,1)}) custom-call(bf16[128,4096]{1,0:T(8,128)(2,1)} %bitcast.13, bf16[128,1024]{1,0:T(8,128)(2,1)} %bitcast.14, bf16[128,1024]{1,0:T(8,128)(2,1)} %bitcast.15, bf16[64,128]{1,0:T(8,128)(2,1)} %e_ref.1, ...), custom_call_target="tpu_custom_call" | custom-call | flops 7247757312 | bytes 3145728 | tf_op jit(solution)/shard_map/attention_contrastive/pallas_call | solution.py:644
  84.2 0.0 copy-start.4
  84.2 0.6 copy-done.4
  84.8 0.5 copy.17
  85.3 0.0 copy-start.1
  85.3 2.3 %copy.18 = bf16[1,128,4096]{2,1,0:T(8,128)(2,1)} copy(bf16[1,128,4096]{2,1,0:T(8,128)(2,1)} %bitcast.10) | data formatting | bytes 2097152
  87.7 0.0 copy-done.1
  87.7 0.0 copy-start
  87.7 0.7 copy.19
  88.4 0.3 copy-done
  88.7 0.7 copy.20
  (1 shorter events, 0.0 us)
Async XLA Ops:
  0.6 0.7 copy-start.2
  1.3 0.7 copy-start.3
  84.2 0.6 copy-start.4
  85.3 2.3 %copy-start.1 = (bf16[128,1024]{1,0:T(8,128)(2,1)S(1)}, bf16[128,1024]{1,0:T(8,128)(2,1)}, u32[]{:S(2)}) copy-start(bf16[128,1024]{1,0:T(8,128)(2,1)} %get-tuple-element.10) | copy-start | bytes 786436
  87.7 1.0 %copy-start = (bf16[128,1024]{1,0:T(8,128)(2,1)S(1)}, bf16[128,1024]{1,0:T(8,128)(2,1)}, u32[]{:S(2)}) copy-start(bf16[128,1024]{1,0:T(8,128)(2,1)} %get-tuple-element.11) | copy-start | bytes 786436

commit v2 on v1

--- a/solution.py
+++ b/solution.py
@@ -37,6 +37,10 @@
     return lax.dot_general(a, b, NT, preferred_element_type=F32)
 
 
+def turned(x):
+    return jnp.transpose(x.astype(F32))
+
+
 def iota(shape, dim):
     return lax.broadcasted_iota(jnp.int32, shape, dim)
 
@@ -62,7 +66,7 @@
     q_ref, k_ref, v_ref, e_ref, qgain_ref, kgain_ref, dlen_ref, slen_ref, ans_ref,
     loss_ref, gq_ref, gk_ref, gv_ref,
     qraw, kraw, vraw, qe, ka, kt, va, vt, qst, qraw_t, qrec, w, ot, ef, sp, sgt, doa, dss, dk, dv,
-    dqb, dkb, dvb, hsend, hrecv, hot_c, hot_t, rsb, zb, pbb, agb, mysc,
+    dqb, dkb, dvb, hsend, hrecv, hot_c, rsb, zb, pbb, agb, mysc, dli, sli, qgi, kgi, ansi,
     kv_s, kv_r, q_s, q_r, h_s, h_r, e_s, e_r, x_s, x_r, c_s, c_r, loc,
     rs_s, rs_r, z_s, z_r, p_s, p_r, a_s, a_r,
     gq_s, gq_r, bh_s, bh_r, bk_s, bk_r,
@@ -83,6 +87,15 @@
             src_ref=src, dst_ref=dst, send_sem=ss, recv_sem=rs, device_id=dev, device_id_type=MESH
         )
 
+    small = [
+        pltpu.make_async_copy(src, dst, loc.at[10 + i])
+        for i, (src, dst) in enumerate(
+            ((dlen_ref, dli), (slen_ref, sli), (qgain_ref, qgi), (kgain_ref, kgi), (ans_ref, ansi))
+        )
+    ]
+    for copy in small:
+        copy.start()
+
     barrier = pltpu.get_barrier_semaphore()
 
     def greet(dev):
@@ -95,16 +108,15 @@
     for k in range(1, NPB):
         greet({"seq": me, "pb": (pb + k) % NPB})
     for zi in range(2):
-        for yi in range(NY):
-            source_z = 2 * y + zi
-
-            @pl.when(jnp.logical_or(source_z != z, yi != y))
+        for k in range(1, NY):
+
+            @pl.when(2 * y + zi != z)
             def _():
-                greet(at(source_z, yi))
+                greet(at(2 * y + zi, (y + k) % NY))
 
     e_yy = z // 2
     e_self = (e_yy == y).astype(jnp.int32)
-    pl.semaphore_wait(barrier, (NY - 1) + (NZ - 1) + (NPB - 1) + NZ - e_self)
+    pl.semaphore_wait(barrier, NY + NZ + NPB - 3 + jnp.where(e_self == 1, 0, NZ - 1))
 
     def kv_copy(dy, g, which):
         src, dst = (k_ref, kraw) if which == 0 else (v_ref, vraw)
@@ -162,11 +174,41 @@
     local[0].start()
     local[1].start()
     order = (2, 1, 3)
-    for g in range(2):
+
+    def kv_start(g):
         for which in range(2):
             for dy in order:
                 kv_copy(dy, g, which).start()
+
+    def q_start(g):
+        for dy in order:
+            q_copy(dy, g).start()
+
+    kv_start(0)
     local[2].start()
+
+    def halo(b, g, which, direction, own=False):
+        buf = kraw if which == 0 else vraw
+        cols = pl.ds(g * 128, 128)
+        dst_row = b * BLOCK + (0 if direction == 0 else 2 * ROWS)
+        if own:
+            src = (k_ref if which == 0 else v_ref).at[:, aligned(y * 256 + g * 128, 128)]
+        else:
+            src = buf.at[aligned(ROWS + b * BLOCK, BLOCK), cols]
+        return remote(
+            src,
+            buf.at[aligned(dst_row, BLOCK), cols],
+            h_s.at[b, g, which, direction],
+            h_r.at[b, g, which, direction],
+            at(up if direction == 0 else down, y),
+        )
+
+    def own_halo(g, which, direction):
+        return halo(y, g, which, direction, True)
+
+    for which in range(2):
+        for direction in range(2):
+            own_halo(0, which, direction).start()
 
     def e_copy(k):
         tz = (z + k) % NZ
@@ -186,15 +228,73 @@
         else:
             e_copy(k).start()
 
-    for g in range(2):
-        for dy in order:
-            q_copy(dy, g).start()
-
-    dfirst_r, dend_r, dfirst_c, dend_c = segments(dlen_ref[...])
-    sfirst_r, send_r, sfirst_c, send_c = segments(slen_ref[...])
-    span_col = column(slen_ref[...])[:, :1]
-    qgain_col = column(qgain_ref[...])[:, :1]
-    kgain = kgain_ref[...]
+    def forward_halos(g):
+        for dy in (1, 3, 2):
+            for which in range(2):
+                kv_landed(dy, g, which).wait_recv()
+                for direction in range(2):
+                    halo((y + NY - dy) % NY, g, which, direction).start()
+
+    def own_halos(g):
+        for which in range(2):
+            for direction in range(2):
+                own_halo(g, which, direction).start()
+
+    kv_start(1)
+    forward_halos(0)
+    q_start(0)
+
+    @pl.when(e_self == 1)
+    def _():
+        local[3].wait()
+
+    for zi in range(2):
+        for yi in range(NY):
+
+            @pl.when(jnp.logical_or(2 * y + zi != z, yi != y))
+            def _():
+                remote(
+                    e_ref, qe.at[pb, :, pl.ds(zi * 512 + yi * 128, 128)], e_s.at[0],
+                    e_r.at[zi, yi], at(2 * y + zi, yi),
+                ).wait_recv()
+
+    def x_copy(k):
+        return remote(
+            qe.at[pb], qe.at[pb], x_s.at[k - 1], x_r.at[k - 1],
+            {"seq": me, "pb": (pb + 2 * k) % NPB},
+        )
+
+    def x_landed(k):
+        src = (pb + NPB - 2 * k) % NPB
+        return remote(
+            qe.at[src], qe.at[src], x_s.at[k - 1], x_r.at[k - 1], {"seq": me, "pb": src}
+        )
+
+    def c_copy(k):
+        part = (pb + NPB - 2 * k) % NPB
+        return remote(
+            qe.at[part], qe.at[part], c_s.at[k], c_r.at[k], {"seq": me, "pb": sibling}
+        )
+
+    def c_landed(k):
+        part = (sibling + NPB - 2 * k) % NPB
+        return remote(
+            qe.at[part], qe.at[part], c_s.at[k], c_r.at[k], {"seq": me, "pb": sibling}
+        )
+
+    for k in (2, 1, 3):
+        x_copy(k).start()
+    c_copy(0).start()
+
+    for copy in small:
+        copy.wait()
+    dlen = jnp.concatenate([dli[...].astype(F32), jnp.zeros((1, 112), F32)], axis=1)
+    slen = sli[...].astype(F32)
+    dfirst_r, dend_r, dfirst_c, dend_c = segments(dlen)
+    sfirst_r, send_r, sfirst_c, send_c = segments(slen)
+    span_col = column(slen)[:, :1]
+    qgain_col = column(qgi[...])[:, :1]
+    kgain = kgi[...]
     base = z * ROWS
     tok_c = (base + iota((SPANS, ROWS), 1)).astype(F32)
     hot_c[...] = jnp.where(
@@ -213,92 +313,37 @@
         ka[g, :, 128:256] = kdoc
         va[g, :, 128:256] = ones_v
     tok_q = (base + iota((128, ROWS), 1)).astype(F32)
-    hot_t[...] = jnp.where(
-        jnp.logical_and(tok_q >= dfirst_c, tok_q < dend_c), 0.0, -MASKED
-    ).astype(BF16)
+    qdoc = jnp.where(jnp.logical_and(tok_q >= dfirst_c, tok_q < dend_c), 0.0, -MASKED).astype(BF16)
+    for r in range(NY):
+        tile = jnp.concatenate([qdoc[:, r * BLOCK : (r + 1) * BLOCK]] * 4, axis=1)
+        for g in range(2):
+            qst[g * NY + r, 128:256, :] = tile
+    doa[:, 128:256, :] = jnp.zeros((NY, 128, 512), BF16)
     sp[...] = jnp.zeros_like(sp)
 
-    def halo(b, g, which, direction):
-        buf = kraw if which == 0 else vraw
-        cols = pl.ds(g * 128, 128)
-        dst_row = b * BLOCK + (0 if direction == 0 else 2 * ROWS)
-        return remote(
-            buf.at[aligned(ROWS + b * BLOCK, BLOCK), cols],
-            buf.at[aligned(dst_row, BLOCK), cols],
-            h_s.at[b, g, which, direction],
-            h_r.at[b, g, which, direction],
-            at(up if direction == 0 else down, y),
-        )
-
-    local[0].wait()
-    local[1].wait()
-    for g in range(2):
-        for which in range(2):
-            for direction in range(2):
-                halo(y, g, which, direction).start()
-        for dy in (1, 3, 2):
-            for which in range(2):
-                kv_landed(dy, g, which).wait_recv()
-                for direction in range(2):
-                    halo((y + NY - dy) % NY, g, which, direction).start()
-
-    @pl.when(e_self == 1)
-    def _():
-        local[3].wait()
-
-    for zi in range(2):
-        for yi in range(NY):
-
-            @pl.when(jnp.logical_or(2 * y + zi != z, yi != y))
-            def _():
-                remote(
-                    e_ref, qe.at[pb, :, pl.ds(zi * 512 + yi * 128, 128)], e_s.at[0],
-                    e_r.at[zi, yi], at(2 * y + zi, yi),
-                ).wait_recv()
-
-    def x_copy(k):
-        return remote(
-            qe.at[pb], qe.at[pb], x_s.at[k - 1], x_r.at[k - 1],
-            {"seq": me, "pb": (pb + 2 * k) % NPB},
-        )
-
-    def x_landed(k):
-        src = (pb + NPB - 2 * k) % NPB
-        return remote(
-            qe.at[src], qe.at[src], x_s.at[k - 1], x_r.at[k - 1], {"seq": me, "pb": src}
-        )
-
-    def c_copy(k):
-        part = (pb + NPB - 2 * k) % NPB
-        return remote(
-            qe.at[part], qe.at[part], c_s.at[k], c_r.at[k], {"seq": me, "pb": sibling}
-        )
-
-    def c_landed(k):
-        part = (sibling + NPB - 2 * k) % NPB
-        return remote(
-            qe.at[part], qe.at[part], c_s.at[k], c_r.at[k], {"seq": me, "pb": sibling}
-        )
-
-    for k in (2, 1, 3):
-        x_copy(k).start()
-    c_copy(0).start()
-
-    local[2].wait()
-    def forward_group(g, _):
+    for copy in local[:3]:
+        copy.wait()
+    def forward_group(g):
         for b in range(NY):
             for which in range(2):
                 for direction in range(2):
                     halo(b, g, which, direction).wait_recv()
+        if g == 0:
+            own_halos(1)
+            forward_halos(1)
+            q_start(1)
         cols = aligned(g * 128, 128)
         key = kraw[:, cols].astype(F32)
-        rec = lax.rsqrt(jnp.mean(key * key, axis=1, keepdims=True) + EPS)
-        key = key * rec * kgain
-        ka[g, :, 0:128] = key.astype(BF16)
-        kt[g] = jnp.transpose(key).astype(BF16)
+        square = key * key
+        high = square.astype(BF16)
+        low = (square - high.astype(F32)).astype(BF16)
+        mean = dot(jnp.concatenate([high, low], axis=1), jnp.ones((256, 128), BF16)) * (1.0 / WIDTH)
+        key = (key * lax.rsqrt(mean + EPS) * kgain).astype(BF16)
+        ka[g, :, 0:128] = key
+        kt[g] = turned(key).astype(BF16)
         val = vraw[:, cols]
         va[g, :, 0:128] = val
-        vt[g] = jnp.transpose(val.astype(F32)).astype(BF16)
+        vt[g] = turned(val).astype(BF16)
 
         def tile(i, _):
             r = (y + i) % NY
@@ -309,16 +354,14 @@
 
             idx = g * NY + r
             rows = aligned(r * BLOCK, BLOCK)
-            x = qraw[rows, aligned(g * 512, 512)].astype(F32)
+            x = qraw[rows, aligned(g * 512, 512)]
             x = jnp.concatenate(
-                [jnp.transpose(x[:, h * 128 : (h + 1) * 128]) for h in range(4)], axis=1
+                [turned(x[:, h * 128 : (h + 1) * 128]) for h in range(4)], axis=1
             )
             qraw_t[idx] = x.astype(BF16)
             rq = lax.rsqrt(jnp.mean(x * x, axis=0, keepdims=True) + EPS)
             qrec[idx] = rq
             qst[idx, 0:128, :] = (x * rq * qgain_col).astype(BF16)
-            qdoc = hot_t[:, rows]
-            qst[idx, 128:256, :] = jnp.concatenate([qdoc] * 4, axis=1)
             rhs = qst[idx]
             total = jnp.zeros((1, 512), F32)
             for c in range(WINDOW // CHUNK):
@@ -340,20 +383,19 @@
             return 0
 
         lax.fori_loop(0, NY, tile, 0)
-        return 0
-
-    lax.fori_loop(0, 2, forward_group, 0)
-
+
+    forward_group(0)
     for k in range(1, 4):
         x_landed(k).wait_recv()
         c_copy(k).start()
+    forward_group(1)
     for k in range(4):
         c_landed(k).wait_recv()
 
     emb = qe[...].reshape(QUERIES, 1024)
     span = (sp[...] / span_col).astype(BF16)
     sims = dot_nt(span, emb)
-    mine = ans_ref[...] - pb * SPANS
+    mine = ansi[...] - pb * SPANS
     span_no = iota((SPANS, QUERIES), 0)
     for j in range(CAND):
         mysc[j : j + 1, :] = jnp.sum(
@@ -379,16 +421,13 @@
         return remote(zb.at[src], zb.at[src], z_s.at[k - 1], z_r.at[k - 1], at(src, y))
 
     def p_copy(k):
-        return remote(
-            pbb.at[pb], pbb.at[pb], p_s.at[k - 1], p_r.at[k - 1],
-            {"seq": me, "pb": (pb + k) % NPB},
-        )
+        dev = {"seq": me, "pb": (pb + k) % NPB}
+        return remote(pbb.at[pb], pbb.at[pb], p_s.at[k - 1], p_r.at[k - 1], dev)
 
     def p_landed(k):
         src = (pb + NPB - k) % NPB
-        return remote(
-            pbb.at[src], pbb.at[src], p_s.at[k - 1], p_r.at[k - 1], {"seq": me, "pb": src}
-        )
+        dev = {"seq": me, "pb": src}
+        return remote(pbb.at[src], pbb.at[src], p_s.at[k - 1], p_r.at[k - 1], dev)
 
     def a_copy(dy):
         ty = (y + dy) % NY
@@ -398,36 +437,35 @@
         sy = (y + NY - dy) % NY
         return remote(agb.at[sy], agb.at[sy], a_s.at[dy - 1], a_r.at[dy - 1], at(z, sy))
 
+    def total_of(buf, count):
+        part = buf[0]
+        for t in range(1, count):
+            part = part + buf[t]
+        return part
+
+    far_first = (4, 3, 5, 2, 6, 1, 7)
     for dy in order:
         rs_copy(dy).start()
     rsb[y] = mysc[:, lanes(y)]
     for dy in order:
         rs_landed(dy).wait_recv()
-    part = rsb[0]
-    for t in range(1, NY):
-        part = part + rsb[t]
-    zb[z] = part
-    for k in (4, 3, 5, 2, 6, 1, 7):
+    zb[z] = total_of(rsb, NY)
+    for k in far_first:
         z_copy(k).start()
-    for k in range(1, NZ):
+    for k in far_first:
         z_landed(k).wait_recv()
-    part = zb[0]
-    for t in range(1, NZ):
-        part = part + zb[t]
-    pbb[pb] = part
-    for k in (4, 3, 5, 2, 6, 1, 7):
+    pbb[pb] = total_of(zb, NZ)
+    for k in far_first:
         p_copy(k).start()
-    for k in range(1, NPB):
+    for k in far_first:
         p_landed(k).wait_recv()
-    part = pbb[0]
-    for t in range(1, NPB):
-        part = part + pbb[t]
-    agb[y] = part
+    agb[y] = total_of(pbb, NPB)
     for dy in order:
         a_copy(dy).start()
     for dy in order:
         a_landed(dy).wait_recv()
-    sims = jnp.concatenate([agb[t] for t in range(NY)], axis=1) / 0.05
+    tiles = [agb[t] for t in range(NY)]
+    sims = jnp.concatenate(tiles, axis=1) / 0.05
     ex = jnp.exp(sims)
     den = jnp.sum(ex, axis=0, keepdims=True)
     loss = jnp.log(den) - sims[0:1, :]
@@ -443,10 +481,10 @@
         dense = dense + jnp.where(span_no == mine[j : j + 1, :], weight[j : j + 1, :], 0.0)
     high = dense.astype(BF16)
     low = (dense - high.astype(F32)).astype(BF16)
-    sg = (dot(high, emb) + dot(low, emb)) / span_col
+    sg = ((dot(high, emb) + dot(low, emb)) / span_col).astype(BF16)
     for h in range(8):
         cols = slice(h * 128, (h + 1) * 128)
-        sgt[cols, :] = jnp.transpose(sg[:, cols]).astype(BF16)
+        sgt[cols, :] = turned(sg[:, cols]).astype(BF16)
 
     def gq_copy(g, r, slot):
         return remote(
@@ -482,13 +520,17 @@
             at(down if direction == 0 else up, y),
         )
 
+    def send_halos(g, which, total, factor):
+        for direction in range(2):
+            first = 2 * ROWS * direction
+            hsend[direction, g, which] = (total[g, first : first + ROWS, :] * factor).astype(BF16)
+            back_halo(g, which, direction).start()
+
     def backward_group(g, _):
         dk[g] = jnp.zeros((3 * ROWS, 128), F32)
         dv[g] = jnp.zeros((3 * ROWS, 128), F32)
 
-        def tile(i, _):
-            off = jnp.where(i == 0, 2, jnp.where(i == 1, 1, jnp.where(i == 2, 3, 0)))
-            r = (y + off) % NY
+        def values_tile(r, _):
             idx = g * NY + r
             rows = aligned(r * BLOCK, BLOCK)
             go = dot(sgt[aligned(g * 512, 512), :], hot_c[:, rows])
@@ -498,17 +540,27 @@
             d0 = delta.astype(BF16).astype(F32)
             d1 = (delta - d0).astype(BF16).astype(F32)
             d2 = delta - d0 - d1
-            row = iota((128, 512), 0)
+            row = iota((16, 512), 0)
             extra = jnp.where(row == 0, -d0, jnp.where(row == 1, -d1, jnp.where(row == 2, -d2, 0.0)))
-            doa[0:128, :] = gob
-            doa[128:256, :] = extra.astype(BF16)
-            rhs = doa[...]
+            doa[r, 0:128, :] = gob
+            doa[r, 128:144, :] = extra.astype(BF16)
+            dv[g, aligned(r * BLOCK, WINDOW), :] += dot_nt(w[idx], gob)
+            return 0
+
+        lax.fori_loop(0, NY, values_tile, 0)
+        send_halos(g, 1, dv, 1.0)
+
+        def tile(i, _):
+            off = jnp.where(i == 0, 2, jnp.where(i == 1, 1, jnp.where(i == 2, 3, 0)))
+            r = (y + off) % NY
+            idx = g * NY + r
+            rows = aligned(r * BLOCK, BLOCK)
+            rhs = doa[r]
             for c in range(WINDOW // CHUNK):
                 dp = dot(va[g, aligned(r * BLOCK + c * CHUNK, CHUNK), :], rhs)
                 part = slice(c * CHUNK, (c + 1) * CHUNK)
                 dss[part, :] = (w[idx, part, :].astype(F32) * dp).astype(BF16)
             window = aligned(r * BLOCK, WINDOW)
-            dv[g, window, :] += dot_nt(w[idx], gob)
             dk[g, window, :] += dot_nt(dss[...], qst[idx, 0:128, :])
             dq = dot(kt[g, :, window], dss[...])
             x = qraw_t[idx].astype(F32)
@@ -517,7 +569,7 @@
             mean = jnp.mean(x * gained, axis=0, keepdims=True)
             res = rq * gained - x * (rq * rq * rq * mean)
             for h in range(4):
-                dqb[rows, aligned(g * 512 + h * 128, 128)] = jnp.transpose(
+                dqb[rows, aligned(g * 512 + h * 128, 128)] = turned(
                     res[:, h * 128 : (h + 1) * 128]
                 ).astype(BF16)
 
@@ -532,13 +584,7 @@
             return 0
 
         lax.fori_loop(0, NY, tile, 0)
-        hsend[0, g, 0] = (dk[g, 0:ROWS, :] * SCALE).astype(BF16)
-        hsend[0, g, 1] = dv[g, 0:ROWS, :].astype(BF16)
-        hsend[1, g, 0] = (dk[g, 2 * ROWS : 3 * ROWS, :] * SCALE).astype(BF16)
-        hsend[1, g, 1] = dv[g, 2 * ROWS : 3 * ROWS, :].astype(BF16)
-        for which in range(2):
-            for direction in range(2):
-                back_halo(g, which, direction).start()
+        send_halos(g, 0, dk, SCALE)
         return 0
 
     lax.fori_loop(0, 2, backward_group, 0)
@@ -576,13 +622,14 @@
     for g in range(2):
         cols = slice(g * 128, (g + 1) * 128)
         for direction in range(2):
-            for which in range(2):
-                back_halo(g, which, direction).wait_recv()
+            back_halo(g, 1, direction).wait_recv()
         vtot = dv[g, ROWS : 2 * ROWS, :] + hrecv[0, g, 1].astype(F32) + hrecv[1, g, 1].astype(F32)
         dvb[:, cols] = vtot.astype(BF16)
         for dy in order:
             bk_copy(dy, g, 1).start()
         bk_local(g, 1).start()
+        for direction in range(2):
+            back_halo(g, 0, direction).wait_recv()
         ktot = (
             dk[g, ROWS : 2 * ROWS, :] * SCALE
             + hrecv[0, g, 0].astype(F32)
@@ -614,26 +661,39 @@
                 for b in range(NY):
                     halo(b, g, which, direction).wait_send()
     for dy in order:
-        rs_copy(dy).wait_send()
-        a_copy(dy).wait_send()
         x_copy(dy).wait_send()
     for k in range(4):
         c_copy(k).wait_send()
     for k in range(1, NZ):
+        e_copy(k).wait_send()
+
+    for dy in order:
+        rs_copy(dy).wait_send()
+        a_copy(dy).wait_send()
+    for k in far_first:
         z_copy(k).wait_send()
         p_copy(k).wait_send()
-        e_copy(k).wait_send()
 
     @pl.when(e_self == 0)
     def _():
         e_copy(0).wait_send()
 
 
+def hand_over(loss_in, gq_in, gk_in, gv_in, loss, gq, gk, gv, sem):
+    copies = [
+        pltpu.make_async_copy(src, dst, sem.at[i])
+        for i, (src, dst) in enumerate(((gq_in, gq), (gk_in, gk), (gv_in, gv)))
+    ]
+    for copy in copies:
+        copy.start()
+    loss[...] = loss_in[0, :]
+    for copy in copies:
+        copy.wait()
+
+
 def on_device(
     queries, keys, values, query_gain, key_gain, doc_lengths, span_lengths, query_emb, answer_options
 ):
-    dlen = jnp.pad(doc_lengths.astype(F32), ((0, 0), (0, 128 - doc_lengths.shape[1])))
-    slen = span_lengths.astype(F32)
     anywhere = pl.BlockSpec(memory_space=pl.ANY)
     vmem = pl.BlockSpec(memory_space=pltpu.VMEM)
 
@@ -644,13 +704,13 @@
     loss, gq, gk, gv = pl.pallas_call(
         body,
         out_shape=(
-            jax.ShapeDtypeStruct((1, QUERIES // NPB), F32),
-            jax.ShapeDtypeStruct((tok, 4096), BF16),
-            jax.ShapeDtypeStruct((tok, 1024), BF16),
-            jax.ShapeDtypeStruct((tok, 1024), BF16),
+            pltpu.VMEM((1, QUERIES // NPB), F32),
+            pltpu.VMEM((tok, 4096), BF16),
+            pltpu.VMEM((tok, 1024), BF16),
+            pltpu.VMEM((tok, 1024), BF16),
         ),
-        in_specs=[anywhere] * 4 + [vmem] * 5,
-        out_specs=(vmem, anywhere, anywhere, anywhere),
+        in_specs=[anywhere] * 9,
+        out_specs=(vmem,) * 4,
         scratch_shapes=[
             pltpu.VMEM((ROWS, 1024), BF16),
             pltpu.VMEM((3 * ROWS, 256), BF16),
@@ -668,7 +728,7 @@
             pltpu.VMEM((WINDOW, 512), F32),
             pltpu.VMEM((SPANS, 1024), F32),
             pltpu.VMEM((1024, SPANS), BF16),
-            pltpu.VMEM((256, 512), BF16),
+            pltpu.VMEM((NY, 256, 512), BF16),
             pltpu.VMEM((WINDOW, 512), BF16),
             pltpu.VMEM((2, 3 * ROWS, 128), F32),
             pltpu.VMEM((2, 3 * ROWS, 128), F32),
@@ -678,19 +738,23 @@
             pltpu.VMEM((2, 2, 2, ROWS, 128), BF16),
             pltpu.VMEM((2, 2, 2, ROWS, 128), BF16),
             pltpu.VMEM((SPANS, ROWS), BF16),
-            pltpu.VMEM((128, ROWS), BF16),
             pltpu.VMEM((NY, 8, 128), F32),
             pltpu.VMEM((NZ, 8, 128), F32),
             pltpu.VMEM((NPB, 8, 128), F32),
             pltpu.VMEM((NY, 8, 128), F32),
             pltpu.VMEM((CAND, QUERIES), F32),
+            pltpu.VMEM((1, 16), jnp.int32),
+            pltpu.VMEM((1, SPANS), jnp.int32),
+            pltpu.VMEM((1, 128), F32),
+            pltpu.VMEM((1, 128), F32),
+            pltpu.VMEM((CAND, QUERIES), jnp.int32),
             dma(3, 2, 2), dma(3, 2, 2),
             dma(3, 2), dma(3, 2),
             dma(NY, 2, 2, 2), dma(NY, 2, 2, 2),
             dma(NZ), dma(2, NY),
             dma(3), dma(3),
             dma(4), dma(4),
-            dma(10),
+            dma(15),
             dma(3), dma(3),
             dma(7), dma(7),
             dma(7), dma(7),
@@ -713,11 +777,24 @@
         query_emb,
         query_gain.reshape(1, 128),
         key_gain.reshape(1, 128),
-        dlen,
-        slen,
+        doc_lengths,
+        span_lengths,
         answer_options.T,
     )
-    return loss.reshape(QUERIES // NPB), gq[None], gk[None], gv[None]
+    loss, gq, gk, gv = pl.pallas_call(
+        hand_over,
+        out_shape=(
+            jax.ShapeDtypeStruct((QUERIES // NPB,), F32),
+            jax.ShapeDtypeStruct((tok, 4096), BF16),
+            jax.ShapeDtypeStruct((tok, 1024), BF16),
+            jax.ShapeDtypeStruct((tok, 1024), BF16),
+        ),
+        in_specs=[vmem] * 4,
+        out_specs=(vmem, anywhere, anywhere, anywhere),
+        scratch_shapes=[dma(3)],
+        name="hand_over",
+    )(*[pltpu.with_memory_space_constraint(part, pltpu.VMEM) for part in (loss, gq, gk, gv)])
+    return loss, gq[None], gk[None], gv[None]
 
 
 def solution(mesh):

time: 89.6 us -> 80.8 us (0.902); the launches traced: 89.4 us -> 79.5 us
  local copies, waits for them, and re-layouts: 6.51 us -> 0 us
  Pallas kernels: 81.7 us -> 78.8 us
    unnamed x14 -> x0, local copies, waits for them, and re-layouts: 5.99 us -> none
    pallas_call x1 -> x2, Pallas kernels: 81.7 us -> 78.8 us  [the longest x1 77.2 us: on_device(): pl.pallas_call(body, out_shape=(pltpu.VMEM((1, QUERIES // NPB), F32), plt...]
where the time goes in v2:
time: 80.8 us; the launch traced here: 79.5 us
  Pallas kernels  78.8 us (98%)
    pallas_call x1, Pallas kernels, on_device(): pl.pallas_call(body, out_shape=(pltpu.VMEM((1, QUERIES // NPB), F32), plt...  77.2 us
    pallas_call x1, Pallas kernels, on_device(): pl.pallas_call(hand_over, out_shape=(jax.ShapeDtypeStruct((QUERIES // NPB...  1.67 us

profile of v2, /device:TPU:2, one launch (start us, length us, event | category | flops | bytes accessed | tf_op | source)
XLA Modules:
  0.0 79.5 jit_solution(11174524925522895825)
XLA Ops:
  0.6 77.2 %attention_contrastive.1 = (f32[1,64]{1,0:T(1,128)S(1)}, bf16[128,4096]{1,0:T(8,128)(2,1)S(1)}, bf16[128,1024]{1,0:T(8,128)(2,1)S(1)}, bf16[128,1024]{1,0:T(8,128)(2,1)S(1)}) custom-call(bf16[128,4096]{1,0:T(8,128)(2,1)} %bitcast.9, bf16[128,1024]{1,0:T(8,128)(2,1)} %bitcast.11, bf16[128,1024]{1,0:T(8,128)(2,1)} %bitcast.12, bf16[64,128]{1,0:T(8,128)(2,1)} %e_ref.1, ...), custom_call_target="tpu_custom_call" | custom-call | flops 7247757312 | bytes 3145728 | tf_op jit(solution)/shard_map/attention_contrastive/pallas_call | solution.py:704
  77.8 1.7 %hand_over.1 = (f32[64]{0:T(128)}, bf16[128,4096]{1,0:T(8,128)(2,1)}, bf16[128,1024]{1,0:T(8,128)(2,1)}, bf16[128,1024]{1,0:T(8,128)(2,1)}) custom-call(f32[1,64]{1,0:T(1,128)S(1)} %get-tuple-element.12.loss_in, bf16[128,4096]{1,0:T(8,128)(2,1)S(1)} %get-tuple-element.13.gq_in, bf16[128,1024]{1,0:T(8,128)(2,1)S(1)} %get-tuple-element.14.gk_in, ...), custom_call_target="tpu_custom_call" | custom-call | tf_op jit(solution)/shard_map/hand_over/pallas_call | solution.py:784

commit v3 on v2

--- a/solution.py
+++ b/solution.py
@@ -65,7 +65,7 @@
 def body(
     q_ref, k_ref, v_ref, e_ref, qgain_ref, kgain_ref, dlen_ref, slen_ref, ans_ref,
     loss_ref, gq_ref, gk_ref, gv_ref,
-    qraw, kraw, vraw, qe, ka, kt, va, vt, qst, qraw_t, qrec, w, ot, ef, sp, sgt, doa, dss, dk, dv,
+    qraw, kv, qe, ka, kt, va, vt, qst, qraw_t, qrec, w, ot, ef, sp, sgt, doa, dss, dk, dv,
     dqb, dkb, dvb, hsend, hrecv, hot_c, rsb, zb, pbb, agb, mysc, dli, sli, qgi, kgi, ansi,
     kv_s, kv_r, q_s, q_r, h_s, h_r, e_s, e_r, x_s, x_r, c_s, c_r, loc,
     rs_s, rs_r, z_s, z_r, p_s, p_r, a_s, a_r,
@@ -119,22 +119,20 @@
     pl.semaphore_wait(barrier, NY + NZ + NPB - 3 + jnp.where(e_self == 1, 0, NZ - 1))
 
     def kv_copy(dy, g, which):
-        src, dst = (k_ref, kraw) if which == 0 else (v_ref, vraw)
         ty = (y + dy) % NY
         return remote(
-            src.at[:, aligned(ty * 256 + g * 128, 128)],
-            dst.at[aligned(ROWS + y * BLOCK, BLOCK), pl.ds(g * 128, 128)],
+            (k_ref if which == 0 else v_ref).at[:, aligned(ty * 256 + g * 128, 128)],
+            kv.at[aligned(ROWS + y * BLOCK, BLOCK), pl.ds(g * 256 + which * 128, 128)],
             kv_s.at[dy - 1, g, which],
             kv_r.at[dy - 1, g, which],
             at(z, ty),
         )
 
     def kv_landed(dy, g, which):
-        src, dst = (k_ref, kraw) if which == 0 else (v_ref, vraw)
         sy = (y + NY - dy) % NY
         return remote(
-            src.at[:, aligned(y * 256 + g * 128, 128)],
-            dst.at[aligned(ROWS + sy * BLOCK, BLOCK), pl.ds(g * 128, 128)],
+            (k_ref if which == 0 else v_ref).at[:, aligned(y * 256 + g * 128, 128)],
+            kv.at[aligned(ROWS + sy * BLOCK, BLOCK), pl.ds(g * 256 + which * 128, 128)],
             kv_s.at[dy - 1, g, which],
             kv_r.at[dy - 1, g, which],
             at(z, sy),
@@ -162,8 +160,14 @@
 
     own_rows = aligned(ROWS + y * BLOCK, BLOCK)
     local = [
-        pltpu.make_async_copy(k_ref.at[:, aligned(y * 256, 256)], kraw.at[own_rows, :], loc.at[0]),
-        pltpu.make_async_copy(v_ref.at[:, aligned(y * 256, 256)], vraw.at[own_rows, :], loc.at[1]),
+        pltpu.make_async_copy(
+            src.at[:, aligned(y * 256 + g * 128, 128)],
+            kv.at[own_rows, pl.ds(g * 256 + which * 128, 128)],
+            loc.at[15 + 2 * g + which],
+        )
+        for g in range(2)
+        for which, src in enumerate((k_ref, v_ref))
+    ] + [
         pltpu.make_async_copy(
             q_ref.at[:, aligned(y * 1024, 1024)], qraw.at[aligned(y * BLOCK, BLOCK), :], loc.at[2]
         ),
@@ -171,8 +175,8 @@
             e_ref, qe.at[pb, :, aligned((z % 2) * 512 + y * 128, 128)], loc.at[3]
         ),
     ]
-    local[0].start()
-    local[1].start()
+    for copy in local[:4]:
+        copy.start()
     order = (2, 1, 3)
 
     def kv_start(g):
@@ -185,30 +189,23 @@
             q_copy(dy, g).start()
 
     kv_start(0)
-    local[2].start()
-
-    def halo(b, g, which, direction, own=False):
-        buf = kraw if which == 0 else vraw
-        cols = pl.ds(g * 128, 128)
+    local[4].start()
+
+    def halo(b, g, direction):
+        cols = pl.ds(g * 256, 256)
         dst_row = b * BLOCK + (0 if direction == 0 else 2 * ROWS)
-        if own:
-            src = (k_ref if which == 0 else v_ref).at[:, aligned(y * 256 + g * 128, 128)]
-        else:
-            src = buf.at[aligned(ROWS + b * BLOCK, BLOCK), cols]
-        return remote(
-            src,
-            buf.at[aligned(dst_row, BLOCK), cols],
-            h_s.at[b, g, which, direction],
-            h_r.at[b, g, which, direction],
+        return remote(
+            kv.at[aligned(ROWS + b * BLOCK, BLOCK), cols],
+            kv.at[aligned(dst_row, BLOCK), cols],
+            h_s.at[b, g, direction],
+            h_r.at[b, g, direction],
             at(up if direction == 0 else down, y),
         )
 
-    def own_halo(g, which, direction):
-        return halo(y, g, which, direction, True)
-
-    for which in range(2):
-        for direction in range(2):
-            own_halo(0, which, direction).start()
+    for copy in local[:4]:
+        copy.wait()
+    for direction in range(2):
+        halo(y, 0, direction).start()
 
     def e_copy(k):
         tz = (z + k) % NZ
@@ -217,7 +214,7 @@
 
     @pl.when(e_self == 1)
     def _():
-        local[3].start()
+        local[5].start()
 
     for k in range(NZ):
         if k == 0:
@@ -232,13 +229,8 @@
         for dy in (1, 3, 2):
             for which in range(2):
                 kv_landed(dy, g, which).wait_recv()
-                for direction in range(2):
-                    halo((y + NY - dy) % NY, g, which, direction).start()
-
-    def own_halos(g):
-        for which in range(2):
             for direction in range(2):
-                own_halo(g, which, direction).start()
+                halo((y + NY - dy) % NY, g, direction).start()
 
     kv_start(1)
     forward_halos(0)
@@ -246,7 +238,7 @@
 
     @pl.when(e_self == 1)
     def _():
-        local[3].wait()
+        local[5].wait()
 
     for zi in range(2):
         for yi in range(NY):
@@ -321,29 +313,33 @@
     doa[:, 128:256, :] = jnp.zeros((NY, 128, 512), BF16)
     sp[...] = jnp.zeros_like(sp)
 
-    for copy in local[:3]:
-        copy.wait()
-    def forward_group(g):
-        for b in range(NY):
-            for which in range(2):
-                for direction in range(2):
-                    halo(b, g, which, direction).wait_recv()
-        if g == 0:
-            own_halos(1)
-            forward_halos(1)
-            q_start(1)
-        cols = aligned(g * 128, 128)
-        key = kraw[:, cols].astype(F32)
+    local[4].wait()
+    def prepare(g, block):
+        rows = slice(block * ROWS, (block + 1) * ROWS)
+        key = kv[rows, g * 256 : g * 256 + 128].astype(F32)
         square = key * key
         high = square.astype(BF16)
         low = (square - high.astype(F32)).astype(BF16)
         mean = dot(jnp.concatenate([high, low], axis=1), jnp.ones((256, 128), BF16)) * (1.0 / WIDTH)
         key = (key * lax.rsqrt(mean + EPS) * kgain).astype(BF16)
-        ka[g, :, 0:128] = key
-        kt[g] = turned(key).astype(BF16)
-        val = vraw[:, cols]
-        va[g, :, 0:128] = val
-        vt[g] = turned(val).astype(BF16)
+        ka[g, rows, 0:128] = key
+        kt[g, :, rows] = turned(key).astype(BF16)
+        val = kv[rows, g * 256 + 128 : g * 256 + 256]
+        va[g, rows, 0:128] = val
+        vt[g, :, rows] = turned(val).astype(BF16)
+
+    def forward_group(g):
+        prepare(g, 1)
+        for b in range(NY):
+            for direction in range(2):
+                halo(b, g, direction).wait_recv()
+        if g == 0:
+            for direction in range(2):
+                halo(y, 1, direction).start()
+            forward_halos(1)
+            q_start(1)
+        prepare(g, 0)
+        prepare(g, 2)
 
         def tile(i, _):
             r = (y + i) % NY
@@ -447,16 +443,38 @@
     for dy in order:
         rs_copy(dy).start()
     rsb[y] = mysc[:, lanes(y)]
+    for g in range(2):
+        for dy in order:
+            q_copy(dy, g).wait_send()
+            for which in range(2):
+                kv_copy(dy, g, which).wait_send()
     for dy in order:
         rs_landed(dy).wait_recv()
     zb[z] = total_of(rsb, NY)
     for k in far_first:
         z_copy(k).start()
+    for g in range(2):
+        for direction in range(2):
+            for b in range(NY):
+                halo(b, g, direction).wait_send()
     for k in far_first:
         z_landed(k).wait_recv()
     pbb[pb] = total_of(zb, NZ)
     for k in far_first:
         p_copy(k).start()
+    for k in range(4):
+        c_copy(k).wait_send()
+    for k in range(1, 4):
+        x_copy(k).wait_send()
+    for k in range(1, NZ):
+        e_copy(k).wait_send()
+
+    @pl.when(e_self == 0)
+    def _():
+        e_copy(0).wait_send()
+
+    dk[...] = jnp.zeros_like(dk)
+    dv[...] = jnp.zeros_like(dv)
     for k in far_first:
         p_landed(k).wait_recv()
     agb[y] = total_of(pbb, NPB)
@@ -527,9 +545,6 @@
             back_halo(g, which, direction).start()
 
     def backward_group(g, _):
-        dk[g] = jnp.zeros((3 * ROWS, 128), F32)
-        dv[g] = jnp.zeros((3 * ROWS, 128), F32)
-
         def values_tile(r, _):
             idx = g * NY + r
             rows = aligned(r * BLOCK, BLOCK)
@@ -588,6 +603,12 @@
         return 0
 
     lax.fori_loop(0, 2, backward_group, 0)
+    for dy in order:
+        rs_copy(dy).wait_send()
+        a_copy(dy).wait_send()
+    for k in far_first:
+        z_copy(k).wait_send()
+        p_copy(k).wait_send()
 
     def bk_copy(dy, g, which):
         ty = (y + dy) % NY
@@ -635,7 +656,7 @@
             + hrecv[0, g, 0].astype(F32)
             + hrecv[1, g, 0].astype(F32)
         )
-        x = kraw[ROWS : 2 * ROWS, cols].astype(F32)
+        x = kv[ROWS : 2 * ROWS, g * 256 : g * 256 + 128].astype(F32)
         rec = lax.rsqrt(jnp.mean(x * x, axis=1, keepdims=True) + EPS)
         gained = kgain * ktot
         mean = jnp.mean(x * gained, axis=1, keepdims=True)
@@ -649,34 +670,13 @@
         for slot, off in enumerate((2, 1, 3)):
             gq_copy(g, (y + off) % NY, slot).wait_send()
             gq_landed(g, (y + NY - off) % NY, slot).wait_recv()
-            q_copy(off, g).wait_send()
         for which in range(2):
             bk_local(g, which).wait()
             for dy in order:
                 bk_copy(dy, g, which).wait_send()
                 bk_landed(dy, g, which).wait_recv()
-                kv_copy(dy, g, which).wait_send()
             for direction in range(2):
                 back_halo(g, which, direction).wait_send()
-                for b in range(NY):
-                    halo(b, g, which, direction).wait_send()
-    for dy in order:
-        x_copy(dy).wait_send()
-    for k in range(4):
-        c_copy(k).wait_send()
-    for k in range(1, NZ):
-        e_copy(k).wait_send()
-
-    for dy in order:
-        rs_copy(dy).wait_send()
-        a_copy(dy).wait_send()
-    for k in far_first:
-        z_copy(k).wait_send()
-        p_copy(k).wait_send()
-
-    @pl.when(e_self == 0)
-    def _():
-        e_copy(0).wait_send()
 
 
 def hand_over(loss_in, gq_in, gk_in, gv_in, loss, gq, gk, gv, sem):
@@ -713,8 +713,7 @@
         out_specs=(vmem,) * 4,
         scratch_shapes=[
             pltpu.VMEM((ROWS, 1024), BF16),
-            pltpu.VMEM((3 * ROWS, 256), BF16),
-            pltpu.VMEM((3 * ROWS, 256), BF16),
+            pltpu.VMEM((3 * ROWS, 512), BF16),
             pltpu.VMEM((NPB, QUERIES // NPB, 1024), BF16),
             pltpu.VMEM((2, 3 * ROWS, 256), BF16),
             pltpu.VMEM((2, 128, 3 * ROWS), BF16),
@@ -750,11 +749,11 @@
             pltpu.VMEM((CAND, QUERIES), jnp.int32),
             dma(3, 2, 2), dma(3, 2, 2),
             dma(3, 2), dma(3, 2),
-            dma(NY, 2, 2, 2), dma(NY, 2, 2, 2),
+            dma(NY, 2, 2), dma(NY, 2, 2),
             dma(NZ), dma(2, NY),
             dma(3), dma(3),
             dma(4), dma(4),
-            dma(15),
+            dma(19),
             dma(3), dma(3),
             dma(7), dma(7),
             dma(7), dma(7),

time: 80.8 us -> 80.4 us (level)
  no operation moved by 1% of the time
where the time goes in v3:
time: 80.4 us; the launch traced here: 79.4 us
  Pallas kernels  78.7 us (98%)
    pallas_call x1, Pallas kernels, on_device(): pl.pallas_call(body, out_shape=(pltpu.VMEM((1, QUERIES // NPB), F32), plt...  77.1 us
    pallas_call x1, Pallas kernels, on_device(): pl.pallas_call(hand_over, out_shape=(jax.ShapeDtypeStruct((QUERIES // NPB...  1.67 us

profile of v3, /device:TPU:2, one launch (start us, length us, event | category | flops | bytes accessed | tf_op | source)
XLA Modules:
  0.0 79.4 jit_solution(12494146261482458534)
XLA Ops:
  0.6 77.1 %attention_contrastive.1 = (f32[1,64]{1,0:T(1,128)S(1)}, bf16[128,4096]{1,0:T(8,128)(2,1)S(1)}, bf16[128,1024]{1,0:T(8,128)(2,1)S(1)}, bf16[128,1024]{1,0:T(8,128)(2,1)S(1)}) custom-call(bf16[128,4096]{1,0:T(8,128)(2,1)} %bitcast.9, bf16[128,1024]{1,0:T(8,128)(2,1)} %bitcast.11, bf16[128,1024]{1,0:T(8,128)(2,1)} %bitcast.12, bf16[64,128]{1,0:T(8,128)(2,1)} %e_ref.1, ...), custom_call_target="tpu_custom_call" | custom-call | flops 7247757312 | bytes 3145728 | tf_op jit(solution)/shard_map/attention_contrastive/pallas_call | solution.py:704
  77.7 1.7 %hand_over.1 = (f32[64]{0:T(128)}, bf16[128,4096]{1,0:T(8,128)(2,1)}, bf16[128,1024]{1,0:T(8,128)(2,1)}, bf16[128,1024]{1,0:T(8,128)(2,1)}) custom-call(f32[1,64]{1,0:T(1,128)S(1)} %get-tuple-element.12.loss_in, bf16[128,4096]{1,0:T(8,128)(2,1)S(1)} %get-tuple-element.13.gq_in, bf16[128,1024]{1,0:T(8,128)(2,1)S(1)} %get-tuple-element.14.gk_in, ...), custom_call_target="tpu_custom_call" | custom-call | tf_op jit(solution)/shard_map/hand_over/pallas_call | solution.py:783

commit v4 on v3

--- a/solution.py
+++ b/solution.py
@@ -342,11 +342,12 @@
         prepare(g, 2)
 
         def tile(i, _):
-            r = (y + i) % NY
+            off = jnp.where(i == 2, 3, jnp.where(i == 3, 2, i))
+            r = (y + off) % NY
 
             @pl.when(i != 0)
             def _():
-                q_landed(NY - i, g).wait_recv()
+                q_landed(NY - off, g).wait_recv()
 
             idx = g * NY + r
             rows = aligned(r * BLOCK, BLOCK)
@@ -603,12 +604,6 @@
         return 0
 
     lax.fori_loop(0, 2, backward_group, 0)
-    for dy in order:
-        rs_copy(dy).wait_send()
-        a_copy(dy).wait_send()
-    for k in far_first:
-        z_copy(k).wait_send()
-        p_copy(k).wait_send()
 
     def bk_copy(dy, g, which):
         ty = (y + dy) % NY
@@ -641,6 +636,13 @@
         )
 
     for g in range(2):
+        if g == 1:
+            for dy in order:
+                rs_copy(dy).wait_send()
+                a_copy(dy).wait_send()
+            for k in far_first:
+                z_copy(k).wait_send()
+                p_copy(k).wait_send()
         cols = slice(g * 128, (g + 1) * 128)
         for direction in range(2):
             back_halo(g, 1, direction).wait_recv()

time: 80.4 us -> 80.5 us (level)
  no operation moved by 1% of the time
where the time goes in v4:
time: 80.5 us; the launch traced here: 79.4 us
  Pallas kernels  78.8 us (98%)
    pallas_call x1, Pallas kernels, on_device(): pl.pallas_call(body, out_shape=(pltpu.VMEM((1, QUERIES // NPB), F32), plt...  77.1 us
    pallas_call x1, Pallas kernels, on_device(): pl.pallas_call(hand_over, out_shape=(jax.ShapeDtypeStruct((QUERIES // NPB...  1.67 us

profile of v4, /device:TPU:2, one launch (start us, length us, event | category | flops | bytes accessed | tf_op | source)
XLA Modules:
  0.0 79.4 jit_solution(2138429214177559799)
XLA Ops:
  0.6 77.1 %attention_contrastive.1 = (f32[1,64]{1,0:T(1,128)S(1)}, bf16[128,4096]{1,0:T(8,128)(2,1)S(1)}, bf16[128,1024]{1,0:T(8,128)(2,1)S(1)}, bf16[128,1024]{1,0:T(8,128)(2,1)S(1)}) custom-call(bf16[128,4096]{1,0:T(8,128)(2,1)} %bitcast.9, bf16[128,1024]{1,0:T(8,128)(2,1)} %bitcast.11, bf16[128,1024]{1,0:T(8,128)(2,1)} %bitcast.12, bf16[64,128]{1,0:T(8,128)(2,1)} %e_ref.1, ...), custom_call_target="tpu_custom_call" | custom-call | flops 7247757312 | bytes 3145728 | tf_op jit(solution)/shard_map/attention_contrastive/pallas_call | solution.py:706
  77.7 1.7 %hand_over.1 = (f32[64]{0:T(128)}, bf16[128,4096]{1,0:T(8,128)(2,1)}, bf16[128,1024]{1,0:T(8,128)(2,1)}, bf16[128,1024]{1,0:T(8,128)(2,1)}) custom-call(f32[1,64]{1,0:T(1,128)S(1)} %get-tuple-element.12.loss_in, bf16[128,4096]{1,0:T(8,128)(2,1)S(1)} %get-tuple-element.13.gq_in, bf16[128,1024]{1,0:T(8,128)(2,1)S(1)} %get-tuple-element.14.gk_in, ...), custom_call_target="tpu_custom_call" | custom-call | tf_op jit(solution)/shard_map/hand_over/pallas_call | solution.py:785
